TPU v7x, 256 devices: a whole 4x4x8 slice. The times are simulated.
256 devices in a mesh: dp: 32 (over x, y, z_hi), tensor: 8 (over z_lo, core).
Axes of the slice: x: 4, y: 4, z: 8 (z_hi: 2, z_lo: 4; z = z_hi * 4 + z_lo), core: 2. Of those that a mesh axis runs over, the one named last changes fastest.
Arguments:
- hidden: bfloat16 [32768, 8192], P(('dp', 'tensor')), may hold values from -24 to 24
- w_key: bfloat16 [8192, 1024], P(None, 'tensor'), may hold values from -0.0625 to 0.0625
- value_weight: bfloat16 [8192, 1024], P(None, 'tensor'), may hold values from -0.0625 to 0.0625
- value_down_factor: bfloat16 [32, 8192], replicated, may hold values from -0.0625 to 0.0625
- value_up_factor: bfloat16 [32, 1024], P(None, 'tensor'), may hold values from -0.5 to 0.5
- mag_value: float32 [1024], P('tensor'), may hold values from 0.5 to 2
- queries: bfloat16 [32768, 4096], P('dp', 'tensor'), may hold values from -1200 to 1200
- grad_attn: bfloat16 [32768, 4096], P('dp', 'tensor'), may hold values from -6 to 6
Outputs:
- grad_hidden: bfloat16 [32768, 8192], P(('dp', 'tensor'))
- grad_down: float32 [32, 8192], P(None, ('dp', 'tensor'))
- grad_up: float32 [32, 1024], P(None, 'tensor')
- grad_mag: float32 [1024], P('tensor')
All inputs are finite; a program needn't handle non-finite values.
Results may differ from a plain program's by a relative error of at most 0.04.
Values may be sent and summed in bfloat16 or wider, within the bound.
No kernel may reach another device: no remote copies, remote signals or barrier semaphores. Data moves between devices by JAX's collectives and lax.ppermute only.
A program may use at most 192 MiB of HBM per device.

v0:
```python
import jax
import jax.numpy as jnp
from jax import lax
from jax.sharding import PartitionSpec as P

HD = 128


adapter_scale = 2.0
rope_base = 500000.0


def rounded_output(values):
    return lax.optimization_barrier(values.astype(jnp.bfloat16))


def rope_tables(length, head_size):
    half_size = head_size // 2
    frequency = rope_base ** (-(jnp.arange(half_size, dtype=jnp.float32) * 2.0 / head_size))
    angles = jnp.arange(length, dtype=jnp.float32)[:, None] * frequency[None, :]
    return (jnp.cos(angles), jnp.sin(angles))


def rotate(vectors, cosine, sine_table, head_size):
    row_count = vectors.shape[0]
    head_count = vectors.shape[1] // head_size
    half_size = head_size // 2
    shaped = vectors.reshape(row_count, head_count, head_size)
    first_half = shaped[:, :, :half_size]
    second_half = shaped[:, :, half_size:]
    cos_part = cosine[:, None, :]
    sin_part = sine_table[:, None, :]
    joined = jnp.concatenate(
        [
            first_half * cos_part - second_half * sin_part,
            second_half * cos_part + first_half * sin_part,
        ],
        axis=2,
    )
    return joined.reshape(row_count, head_count * head_size)


def unrotate(gradients, cosine, sine_table, head_size):
    row_count = gradients.shape[0]
    head_count = gradients.shape[1] // head_size
    half_size = head_size // 2
    shaped = gradients.reshape(row_count, head_count, head_size)
    first_half = shaped[:, :, :half_size]
    second_half = shaped[:, :, half_size:]
    cos_part = cosine[:, None, :]
    sin_part = sine_table[:, None, :]
    joined = jnp.concatenate(
        [
            first_half * cos_part + second_half * sin_part,
            second_half * cos_part - first_half * sin_part,
        ],
        axis=2,
    )
    return joined.reshape(row_count, head_count * head_size)


def attend_head(query_group, grad_group, key_head, value_head, inv_sqrt):
    length = key_head.shape[0]
    block_rows = min(512, length)
    key_grad = jnp.zeros(key_head.shape, jnp.float32)
    value_grad = jnp.zeros(value_head.shape, jnp.float32)
    for row_start in range(0, length, block_rows):
        row_stop = row_start + block_rows
        query_block = query_group[row_start:row_stop]
        grad_block = grad_group[row_start:row_stop]
        key_part = key_head[:row_stop]
        value_part = value_head[:row_stop]
        scores = (
            jnp.einsum(
                "qgd,kd->gqk",
                query_block.astype(jnp.float32),
                key_part,
                precision=lax.Precision.HIGHEST,
            )
            * inv_sqrt
        )
        row_index = row_start + jnp.arange(block_rows)
        key_index = jnp.arange(row_stop)
        allowed = key_index[None, :] <= row_index[:, None]
        scores = jnp.where(allowed[None], scores, -1e30)
        attn_probs = jax.nn.softmax(scores, axis=-1)
        attn_half = attn_probs.astype(jnp.bfloat16)
        outputs = jnp.einsum(
            "gqk,kd->gqd", attn_half, value_part, preferred_element_type=jnp.float32
        )
        row_delta = jnp.sum(
            jnp.transpose(grad_block, (1, 0, 2)).astype(jnp.float32) * outputs, axis=-1
        )
        probs_grad = jnp.einsum(
            "qgd,kd->gqk", grad_block, value_part, preferred_element_type=jnp.float32
        )
        scores_grad = (attn_probs * (probs_grad - row_delta[:, :, None]) * inv_sqrt).astype(
            jnp.bfloat16
        )
        key_grad = key_grad.at[:row_stop].add(
            jnp.einsum("gqk,qgd->kd", scores_grad, query_block, preferred_element_type=jnp.float32)
        )
        value_grad = value_grad.at[:row_stop].add(
            jnp.einsum("gqk,qgd->kd", attn_half, grad_block, preferred_element_type=jnp.float32)
        )
    return (key_grad, value_grad)


def shards(
    hidden, w_key, value_weight, value_down_factor, value_up_factor, mag_value, queries, grad_attn
):
    tensor_count = lax.axis_size("tensor")
    tok_local = hidden.shape[0]
    length = tok_local * tensor_count
    head_size = HD
    inv_sqrt = head_size ** (-0.5)
    local_width = w_key.shape[1]
    group_size = queries.shape[1] // local_width
    cosine, sine_table = rope_tables(length, head_size)
    low_rank_update = jnp.dot(
        value_down_factor.T, value_up_factor, preferred_element_type=jnp.float32
    )
    merged_weight = value_weight.astype(jnp.float32) + adapter_scale * low_rank_update
    col_norms = jnp.sqrt(jnp.sum(merged_weight * merged_weight, axis=0))
    col_scale = mag_value / col_norms
    piece_rows = lax.all_gather(hidden, "tensor", axis=0, tiled=True)
    key_term = jnp.dot(piece_rows, w_key, preferred_element_type=jnp.float32)
    value_term = jnp.dot(piece_rows, value_weight, preferred_element_type=jnp.float32)
    down_piece = jnp.einsum(
        "td,rd->tr", piece_rows, value_down_factor, preferred_element_type=jnp.float32
    )
    joined = jnp.concatenate([key_term, value_term, down_piece], axis=1)
    key_proj = joined[:, :local_width]
    down_projection = rounded_output(joined[:, 2 * local_width :])
    base_value = rounded_output(
        joined[:, local_width : 2 * local_width]
        + adapter_scale
        * jnp.dot(down_projection, value_up_factor, preferred_element_type=jnp.float32)
    )
    key_rot = rotate(key_proj, cosine, sine_table, head_size)
    value_heads = (col_scale * base_value.astype(jnp.float32)).astype(jnp.bfloat16)
    key_grad, value_grad = attend_head(
        queries.reshape(length, group_size, head_size),
        grad_attn.reshape(length, group_size, head_size),
        key_rot,
        value_heads,
        inv_sqrt,
    )
    value_list = value_grad
    value_grad = value_list
    grad_key = unrotate(key_grad, cosine, sine_table, head_size).astype(jnp.bfloat16)
    value_gradient = (value_grad * col_scale).astype(jnp.bfloat16)
    mag_term = jnp.sum(value_grad * base_value.astype(jnp.float32), axis=0) / col_norms
    right_piece = adapter_scale * jnp.einsum(
        "sr,sh->rh", down_projection, value_gradient, preferred_element_type=jnp.float32
    )
    right_sum, mag_sum = lax.psum((right_piece, mag_term), "dp")
    rank_part = jnp.einsum(
        "sh,rh->sr", value_gradient, value_up_factor, preferred_element_type=jnp.float32
    )
    rank_sum = lax.psum_scatter(
        rank_part.astype(jnp.bfloat16), "tensor", scatter_dimension=0, tiled=True
    )
    row_sum_total = lax.psum_scatter(
        (
            jnp.einsum("th,dh->td", grad_key, w_key, preferred_element_type=jnp.float32)
            + jnp.einsum(
                "th,dh->td", value_gradient, value_weight, preferred_element_type=jnp.float32
            )
        ).astype(jnp.bfloat16),
        "tensor",
        scatter_dimension=0,
        tiled=True,
    ).astype(jnp.float32)
    grad_hidden = (
        row_sum_total
        + adapter_scale * jnp.dot(rank_sum, value_down_factor, preferred_element_type=jnp.float32)
    ).astype(jnp.bfloat16)
    down_piece = adapter_scale * jnp.einsum(
        "tr,td->rd", rank_sum, hidden, preferred_element_type=jnp.float32
    )
    down_sum = lax.psum_scatter(down_piece, ("dp", "tensor"), scatter_dimension=1, tiled=True)
    return (grad_hidden, down_sum, right_sum, mag_sum)


def solution(mesh):
    return jax.shard_map(
        shards,
        mesh=mesh,
        in_specs=(
            P(("dp", "tensor"), None),
            P(None, "tensor"),
            P(None, "tensor"),
            P(),
            P(None, "tensor"),
            P("tensor"),
            P("dp", "tensor"),
            P("dp", "tensor"),
        ),
        out_specs=(
            P(("dp", "tensor"), None),
            P(None, ("dp", "tensor")),
            P(None, "tensor"),
            P("tensor"),
        ),
        check_vma=False,
    )
```

profile of v0, /device:TPU:1, one launch (start us, length us, event | category | flops | bytes accessed | tf_op | source)
XLA Modules:
  0.0 1739.1 jit_solution(10532708551808847547)
XLA Ops:
  7.2 0.0 copy-start
  7.2 0.0 all-gather.2.cloned.1.call-start
  7.2 0.7 all-gather.2.cloned.1.call-update
  7.9 0.0 copy-start.4
  7.9 0.0 copy-start.14
  7.9 0.0 reduce-scatter.10.cloned.1.call-start
  8.0 2.1 fusion.70
  10.1 1.0 copy.70
  11.1 1.3 copy.72
  12.4 2.3 fusion.69
  14.6 2.1 copy.71
  16.7 2.0 copy.73
  18.7 0.1 iota_compare_fusion.1
  18.8 0.0 copy-done.4
  18.8 0.0 copy-done.14
  18.8 2.9 fusion.26
  21.7 0.0 copy-done.15
  21.7 1.2 iota_compare_fusion
  22.9 161.0 %all-gather.2.cloned.1.call-done = bf16[1024,8192]{1,0:T(8,128)(2,1)} async-done(((bf16[128,8192]{1,0:T(8,128)(2,1)}), bf16[1024,8192]{1,0:T(8,128)(2,1)}) %all-gather.2.cloned.1.call-update) | async-done | bytes 16777232 | tf_op jit(solution)/shard_map/all_gather | solution.py:126
  183.9 11.0 convolution_convert_fusion
  194.9 0.0 copy-done.1
  194.9 6.1 fusion.73
  201.0 1.0 fusion.41
  202.0 0.0 copy-done
  202.0 12.7 convolution_bitcast_fusion
  214.7 2.1 multiply_subtract_fusion
  216.9 0.0 copy-done.6
  216.9 1.9 fusion.50
  218.8 3.6 fusion.44
  222.4 2.1 fusion.72
  224.6 1.9 copy-done.2
  226.5 0.6 fusion.25
  227.1 0.0 copy-done.7
  227.2 0.7 convolution_bitcast_fusion.2
  227.9 6.4 fusion.71
  234.3 4.6 fusion.18
  239.0 1.3 fusion.47
  240.3 0.8 fusion.28
  241.1 0.0 copy-done.16
  241.1 0.5 fusion.29
  241.6 4.5 fusion.42
  246.1 0.2 convolution_convert_fusion.1
  246.3 0.9 copy.66
  247.2 0.0 reduce-scatter.10.cloned.1.call-update
  247.2 0.0 reduce-scatter.12.cloned.1.call-start
  247.3 6.6 fusion.37
  253.8 1.8 add_convert_fusion.1
  255.7 25.2 %reduce-scatter.10.cloned.1.call-done = bf16[128,32]{1,0:T(8,128)(2,1)} async-done(((bf16[1024,32]{1,0:T(8,128)(2,1)}), bf16[128,32]{1,0:T(8,128)(2,1)}) %reduce-scatter.10.cloned.1.call-update) | async-done | bytes 8208
  280.9 2.1 convolution_multiply_fusion.2
  282.9 2.7 copy.68
  285.7 0.0 reduce-scatter.12.cloned.1.call-update
  285.7 0.0 reduce-scatter.8.cloned.1.call-start
  285.7 0.8 copy-done.8
  286.6 0.1 copy-done.9
  286.6 13.3 fusion.52
  299.9 19.0 %add_convert_fusion = bf16[1024,8192]{1,0:T(8,128)(2,1)} fusion(f32[1024,8192]{1,0:T(8,128)} %fusion.52, bf16[1024,128]{1,0:T(8,128)(2,1)S(1)} %get-tuple-element.79, bf16[8192,128]{1,0:T(8,128)(2,1)S(1)} %copy-done.3), kind=kOutput, calls=%fused_computation.2 | convolution fusion | flops 2164260864 | bytes 52690944 | tf_op jit(solution)/shard_map/th,dh->td/dot_general | solution.py:167
  318.9 0.0 reduce-scatter.8.cloned.1.call-update
  318.9 0.2 convolution_multiply_fusion.6
  319.1 197.3 %all-reduce.2 = (f32[32,128]{1,0:T(8,128)}, f32[128]{0:T(128)}) all-reduce(f32[32,128]{1,0:T(8,128)S(1)} %convolution_multiply_fusion.6, f32[128]{0:T(128)S(1)} %sqrt_divide_fusion), channel_id=1, replica_groups=mesh['dp'=32,'tensor'=8] {'dp'}, use_global_device_ids=true, to_apply=%region_10.11 | all-reduce | flops 4224 | bytes 33792 | tf_op jit(solution)/shard_map/psum | solution.py:157
  516.4 1040.8 %reduce-scatter.12.cloned.1.call-done = f32[32,32]{1,0:T(8,128)} async-done(((f32[8192,32]{1,0:T(8,128)}), f32[32,32]{1,0:T(8,128)}) %reduce-scatter.12.cloned.1.call-update) | async-done | bytes 4112
  1557.3 1.4 copy.69
  1558.7 170.1 %reduce-scatter.8.cloned.1.call-done = bf16[128,8192]{1,0:T(8,128)(2,1)} async-done(((bf16[1024,8192]{1,0:T(8,128)(2,1)}), bf16[128,8192]{1,0:T(8,128)(2,1)}) %reduce-scatter.8.cloned.1.call-update) | async-done | bytes 2097168 | tf_op jit(solution)/shard_map/reduce_scatter | solution.py:164
  1728.8 0.0 copy-done.13
  1728.8 3.6 fusion.5
  (23 shorter events, 0.1 us)
Async XLA Ops:
  7.2 194.8 %copy-start = (bf16[8192,128]{1,0:T(8,128)(2,1)S(1)}, bf16[8192,128]{1,0:T(8,128)(2,1)}, u32[]{:S(2)}) copy-start(bf16[8192,128]{1,0:T(8,128)(2,1)} %param.21) | copy-start | bytes 6291460
  7.2 176.8 %all-gather.2.cloned.1.call-start = ((), (), s32[]{:S(2)}) async-start(), calls=%async_computation.3 | async-start | bytes 18874368 | tf_op jit(solution)/shard_map/all_gather | solution.py:126
  7.9 10.9 copy-start.4
  7.9 10.9 copy-start.14
  7.9 272.9 %reduce-scatter.10.cloned.1.call-start = ((), (), s32[]{:S(2)}) async-start(), calls=%async_computation.5 | async-start | bytes 294912
  14.6 7.1 copy-start.15
  183.9 11.0 copy-start.1
  202.0 14.9 copy-start.6
  224.5 2.0 copy-start.2
  224.6 2.6 copy-start.7
  226.5 1.4 copy-start.11
  234.3 4.7 copy-start.10
  234.3 4.7 copy-start.12
  240.3 0.8 copy-start.16
  247.2 1310.1 %reduce-scatter.12.cloned.1.call-start = ((), (), s32[]{:S(2)}) async-start(), calls=%async_computation.6 | async-start | bytes 4210688
  285.7 0.9 copy-start.8
  285.7 1.0 copy-start.9
  285.7 1443.1 %reduce-scatter.8.cloned.1.call-start = ((), (), s32[]{:S(2)}) async-start(), calls=%async_computation.4 | async-start | bytes 18874368 | tf_op jit(solution)/shard_map/reduce_scatter | solution.py:164
  286.6 13.3 copy-start.3
  318.9 1409.9 %copy-start.5 = (bf16[32,8192]{1,0:T(8,128)(2,1)S(1)}, bf16[32,8192]{1,0:T(8,128)(2,1)}, u32[]{:S(2)}) copy-start(bf16[32,8192]{1,0:T(8,128)(2,1)} %param.23) | copy-start | bytes 1572868
  318.9 1409.9 %copy-start.13 = (bf16[128,32]{1,0:T(8,128)(2,1)S(1)}, bf16[128,32]{1,0:T(8,128)(2,1)}, u32[]{:S(2)}) copy-start(bf16[128,32]{1,0:T(8,128)(2,1)} %reduce-scatter.10.cloned.1.call-done) | copy-start | bytes 24580
Sparse Core Ops, SparseCore 0:
  9.8 174.0 all-gather.1
  247.3 33.5 reduce-scatter.9
  285.8 1271.4 reduce-scatter.11
  1559.7 168.9 reduce-scatter.7
where the time goes:
time: 1750 us; the launch traced here: 1740 us
  waiting for transfers between devices  1400 us (80%)
  blocking collectives  197 us (11%)
  matrix products  91.8 us (5%)
  other arithmetic  19.1 us (1%)
  local copies, waits for them, and re-layouts  18.6 us (1%)
    unnamed x6, waiting for transfers between devices  1070 us
    psum x1, blocking collectives, shards(): right_sum, mag_sum = lax.psum((right_piece, mag_term), 'dp')  197 us
    reduce_scatter x1, waiting for transfers between devices, shards(): lax.psum_scatter((jnp.einsum('th,dh->td', grad_key, w_key, preferred_elem...  170 us
    all_gather x1, waiting for transfers between devices, shards(): piece_rows = lax.all_gather(hidden, 'tensor', axis=0, tiled=True)  161 us
  transfers between devices with their start and end apart: 4, of which 4 were waited for; matrix products, arithmetic and copies ran while one was open for 3% of the time, Pallas kernels for 0%

commit v1 on v0

v1 whole, which is shorter than its diff:
```python
import jax
import jax.numpy as jnp
import numpy as np
from jax import lax
from jax.experimental import pallas as pl
from jax.experimental.pallas import tpu as pltpu
from jax.sharding import Mesh, PartitionSpec as P

HD = 128
D = 8192
SEQ = 1024
RANK = 32
PAIR = 256
KB = 512
QB = 256
GROUP = 4
SCALE = 2.0
ROPE_BASE = 500000.0
LOG2E = 1.4426950408889634
INV_SQRT = HD ** (-0.5)
MIB = 1024 * 1024
BF = jnp.bfloat16
F32 = jnp.float32
NT = (((1,), (1,)), ((), ()))
TN = (((0,), (0,)), ((), ()))
EVERY = ("x", "y", "zh", "zl", "core")
DP = ("x", "y", "zh")


def rope_tables():
    half = HD // 2
    frequency = ROPE_BASE ** (-(jnp.arange(half, dtype=F32) * 2.0 / HD))
    angles = jnp.arange(SEQ, dtype=F32)[:, None] * frequency[None, :]
    cosine, sine = jnp.cos(angles), jnp.sin(angles)
    return jnp.concatenate([cosine, cosine], 1), jnp.concatenate([-sine, sine], 1)


def smem():
    return pl.BlockSpec(memory_space=pltpu.SMEM)


def whole(shape):
    return pl.BlockSpec(shape, lambda *_: (0,) * len(shape))


def params(limit):
    return pltpu.CompilerParams(vmem_limit_bytes=limit * MIB)


def cost(flops, moved, trans=0):
    return pl.CostEstimate(flops=flops, bytes_accessed=moved, transcendentals=trans)


def project_kernel(place, hid, own_key, own_val, far, down, ups, cos, sin, out, acc):
    step = pl.program_id(0)

    @pl.when(step == 0)
    def _():
        acc[...] = jnp.zeros_like(acc)

    rows = hid[...]
    own = jnp.concatenate([own_key[...], own_val[...]], axis=1)
    acc[0] += jnp.dot(rows, own, preferred_element_type=F32)
    for r in range(1, 4):
        acc[r] += jnp.dot(rows, far[:, (r - 1) * 256 : r * 256], preferred_element_type=F32)

    @pl.when(step == pl.num_programs(0) - 1)
    def _():
        for r in range(4):
            key = acc[r, :, :HD]
            turned = key * cos[...] + pltpu.roll(key, HD // 2, 1) * sin[...]
            turned = turned * (INV_SQRT * LOG2E)
            high = turned.astype(BF)
            low = (turned - high.astype(F32)).astype(BF)
            lifted = jnp.dot(down[...], ups[r], preferred_element_type=F32)
            base = (acc[r, :, HD:] + SCALE * lifted).astype(BF)
            slot = lax.rem(place[0] + r, 4)
            out[slot] = jnp.concatenate([high, low, base], axis=1)


def project(place, pair, w_key, w_val, far, down, ups, cos, sin):
    return pl.pallas_call(
        project_kernel,
        grid=(D // KB,),
        in_specs=[
            smem(),
            pl.BlockSpec((PAIR, KB), lambda k: (0, k)),
            pl.BlockSpec((KB, HD), lambda k: (k, 0)),
            pl.BlockSpec((KB, HD), lambda k: (k, 0)),
            pl.BlockSpec((KB, 6 * HD), lambda k: (k, 0)),
            whole((PAIR, RANK)),
            whole((4, RANK, HD)),
            whole((PAIR, HD)),
            whole((PAIR, HD)),
        ],
        out_specs=whole((4, PAIR, 3 * HD)),
        out_shape=jax.ShapeDtypeStruct((4, PAIR, 3 * HD), BF),
        scratch_shapes=[pltpu.VMEM((4, PAIR, 2 * HD), F32)],
        compiler_params=params(32),
        cost_estimate=cost(2 * PAIR * D * 1024, 20 * MIB),
        name="project",
    )(place, pair, w_key, w_val, far, down, ups, cos, sin)


def attend_kernel(query, grad, rows, col_scale, down, cos, sin, grads, up_grad, mag_grad, vals, dkey, dval):
    head = pl.program_id(0)

    @pl.when(head == 0)
    def _():
        vals[...] = (rows[:, 2 * HD :].astype(F32) * col_scale[...]).astype(BF)
        dkey[...] = jnp.zeros_like(dkey)
        dval[...] = jnp.zeros_like(dval)

    for block in range(SEQ // QB):
        stop = (block + 1) * QB
        here = slice(block * QB, stop)
        q = query[here, :]
        g = grad[here, :]
        qq = jnp.concatenate([q, q], axis=1)
        scores = lax.dot_general(rows[:stop, : 2 * HD], qq, NT, preferred_element_type=F32)
        key_at = lax.broadcasted_iota(jnp.int32, (QB, QB), 0)
        query_at = lax.broadcasted_iota(jnp.int32, (QB, QB), 1)
        edge = jnp.where(key_at <= query_at, scores[block * QB :], -1e30)
        if block:
            scores = jnp.concatenate([scores[: block * QB], edge], axis=0)
        else:
            scores = edge
        powers = jnp.exp2(scores - jnp.max(scores, axis=0, keepdims=True))
        attn = powers * (1.0 / jnp.sum(powers, axis=0, keepdims=True))
        half = attn.astype(BF)
        pgrad = lax.dot_general(vals[:stop], g, NT, preferred_element_type=F32)
        delta = jnp.sum(half.astype(F32) * pgrad, axis=0, keepdims=True)
        sgrad = (attn * (pgrad - delta)).astype(BF)
        dval[:stop] += jnp.dot(half, g, preferred_element_type=F32)
        dkey[:stop] += jnp.dot(sgrad, q, preferred_element_type=F32)

    @pl.when(head == pl.num_programs(0) - 1)
    def _():
        dk = dkey[...] * INV_SQRT
        dk = dk * cos[...] - pltpu.roll(dk, HD // 2, 1) * sin[...]
        dv = dval[...]
        gv = (dv * col_scale[...]).astype(BF)
        grads[:, :HD] = dk.astype(BF)
        grads[:, HD:] = gv
        up_grad[...] = SCALE * lax.dot_general(down[...], gv, TN, preferred_element_type=F32)
        total = jnp.sum(dv * rows[:, 2 * HD :].astype(F32), axis=0, keepdims=True)
        mag_grad[...] = jnp.broadcast_to(total, mag_grad.shape)


def attend(queries, grad_attn, rows, col_scale, down, cos, sin):
    return pl.pallas_call(
        attend_kernel,
        grid=(GROUP,),
        in_specs=[
            pl.BlockSpec((SEQ, HD), lambda h: (0, h)),
            pl.BlockSpec((SEQ, HD), lambda h: (0, h)),
            whole((SEQ, 3 * HD)),
            whole((1, HD)),
            whole((SEQ, RANK)),
            whole((SEQ, HD)),
            whole((SEQ, HD)),
        ],
        out_specs=[whole((SEQ, 2 * HD)), whole((RANK, HD)), whole((8, HD))],
        out_shape=[
            jax.ShapeDtypeStruct((SEQ, 2 * HD), BF),
            jax.ShapeDtypeStruct((RANK, HD), F32),
            jax.ShapeDtypeStruct((8, HD), F32),
        ],
        scratch_shapes=[
            pltpu.VMEM((SEQ, HD), BF),
            pltpu.VMEM((SEQ, HD), F32),
            pltpu.VMEM((SEQ, HD), F32),
        ],
        compiler_params=params(40),
        cost_estimate=cost(5 * 2 * GROUP * SEQ * SEQ * HD, 6 * MIB, GROUP * SEQ * SEQ),
        name="attend",
    )(queries, grad_attn, rows, col_scale, down, cos, sin)


def rank_kernel(place, grads, ups, out):
    total = jnp.zeros((PAIR, RANK), F32)
    for r in range(4):
        slot = lax.rem(place[0] + r, 4)
        total += lax.dot_general(grads[slot, :, HD:], ups[r], NT, preferred_element_type=F32)
    out[...] = total


def rank_part(place, grads, ups):
    return pl.pallas_call(
        rank_kernel,
        in_specs=[smem(), whole((4, PAIR, 2 * HD)), whole((4, RANK, HD))],
        out_specs=whole((PAIR, RANK)),
        out_shape=jax.ShapeDtypeStruct((PAIR, RANK), F32),
        compiler_params=params(16),
        cost_estimate=cost(2 * PAIR * 512 * RANK, MIB),
        name="rank_part",
    )(place, grads, ups)


def back_kernel(place, grads, own_key, own_val, far, mine, theirs, left):
    step = pl.program_id(0)

    @pl.when(step == 0)
    def _():
        first = pl.multiple_of(place[1] * 128, 128)
        second = pl.multiple_of(128 - place[1] * 128, 128)
        for r in range(4):
            slot = lax.rem(place[0] + r, 4)
            left[:128, r * 256 : (r + 1) * 256] = grads[slot, pl.ds(first, 128), :]
            left[128:, r * 256 : (r + 1) * 256] = grads[slot, pl.ds(second, 128), :]

    weights = jnp.concatenate([own_key[...], own_val[...], far[...]], axis=1)
    part = lax.dot_general(left[...], weights, NT, preferred_element_type=F32)
    mine[...] = part[:128]
    theirs[...] = part[128:].astype(BF)


def back(place, grads, w_key, w_val, far):
    return pl.pallas_call(
        back_kernel,
        grid=(D // KB,),
        in_specs=[
            smem(),
            whole((4, PAIR, 2 * HD)),
            pl.BlockSpec((KB, HD), lambda k: (k, 0)),
            pl.BlockSpec((KB, HD), lambda k: (k, 0)),
            pl.BlockSpec((KB, 6 * HD), lambda k: (k, 0)),
        ],
        out_specs=[
            pl.BlockSpec((128, KB), lambda k: (0, k)),
            pl.BlockSpec((128, KB), lambda k: (0, k)),
        ],
        out_shape=[jax.ShapeDtypeStruct((128, D), F32), jax.ShapeDtypeStruct((128, D), BF)],
        scratch_shapes=[pltpu.VMEM((PAIR, 1024), BF)],
        compiler_params=params(32),
        cost_estimate=cost(2 * PAIR * D * 1024, 23 * MIB),
        name="back",
    )(place, grads, w_key, w_val, far)


def down_kernel(place, rank, hid, out):
    part = SCALE * lax.dot_general(rank[...], hid[...], TN, preferred_element_type=F32)
    lane = lax.broadcasted_iota(jnp.int32, (8, HD), 1) // 32
    core = place[1]
    for tile in range(part.shape[1] // HD):
        regs = [part[8 * i : 8 * i + 8, tile * HD : (tile + 1) * HD] for i in range(4)]
        for pick in range(2):
            column = 2 * pick + core
            block = jnp.zeros((8, HD), F32)
            for i in range(4):
                moved = pltpu.roll(regs[i], lax.rem((i - column + 4) * 32, HD), 1)
                block = jnp.where(lane == i, moved, block)
            out[2 * tile + pick] = block


def down_part(place, rank, pair):
    wide = 1024
    return pl.pallas_call(
        down_kernel,
        grid=(D // wide,),
        in_specs=[smem(), whole((PAIR, RANK)), pl.BlockSpec((PAIR, wide), lambda k: (0, k))],
        out_specs=pl.BlockSpec((wide // 64, 8, HD), lambda k: (k, 0, 0)),
        out_shape=jax.ShapeDtypeStruct((128, 8, HD), F32),
        compiler_params=params(16),
        cost_estimate=cost(2 * PAIR * D * RANK, 5 * MIB),
        name="down_part",
    )(place, rank, pair)


def join_kernel(place, rank, mine, theirs, factor, out):
    own = rank[pl.ds(pl.multiple_of(place[1] * 128, 128), 128), :]
    adapter = SCALE * jnp.dot(own, factor[...], preferred_element_type=F32)
    out[...] = (mine[...] + theirs[...].astype(F32) + adapter).astype(BF)


def join(place, rank, mine, theirs, factor):
    wide = 2048
    return pl.pallas_call(
        join_kernel,
        grid=(D // wide,),
        in_specs=[
            smem(),
            whole((PAIR, RANK)),
            pl.BlockSpec((128, wide), lambda k: (0, k)),
            pl.BlockSpec((128, wide), lambda k: (0, k)),
            pl.BlockSpec((RANK, wide), lambda k: (0, k)),
        ],
        out_specs=pl.BlockSpec((128, wide), lambda k: (0, k)),
        out_shape=jax.ShapeDtypeStruct((128, D), BF),
        compiler_params=params(16),
        cost_estimate=cost(2 * 128 * RANK * D, 9 * MIB),
        name="join",
    )(place, rank, mine, theirs, factor)


def gather_weights(w_key, w_val, up):
    at = (lax.axis_index("x") * 4 + lax.axis_index("y")) * 512
    seed = jnp.concatenate(
        [lax.dynamic_slice(w_key, (at, 0), (512, HD)), lax.dynamic_slice(w_val, (at, 0), (512, HD))], axis=1
    )
    seed = jnp.concatenate([seed, jnp.pad(up, ((0, 0), (0, HD)))], axis=0)
    got = []
    for shift in (-1, -2, 1):
        got.append(lax.ppermute(seed, ("zh", "zl"), [(i, (i + shift) % 8) for i in range(8)]))
    far = lax.all_gather(jnp.concatenate([g[:512] for g in got], axis=1), ("x", "y"), axis=0, tiled=True)
    ups = jnp.stack([up] + [g[512:, :HD] for g in got])
    return far, ups


def shards(hidden, w_key, w_val, factor, up, mag, queries, grad_attn):
    zl, core = lax.axis_index("zl"), lax.axis_index("core")
    place = jnp.stack([zl, core]).astype(jnp.int32)
    swap = [(0, 1), (1, 0)]
    far, ups = gather_weights(w_key, w_val, up)
    other = lax.ppermute(hidden, "core", swap)
    pair = jnp.where(
        core == 0, jnp.concatenate([hidden, other], axis=0), jnp.concatenate([other, hidden], axis=0)
    )
    down = lax.dot_general(pair, factor, NT, preferred_element_type=F32).astype(BF)
    all_down = lax.all_to_all(
        jnp.broadcast_to(down[None], (4, PAIR, RANK)), "zl", 0, 0, tiled=True
    ).reshape(SEQ, RANK)
    merged = w_val.astype(F32) + SCALE * lax.dot_general(factor, up, TN, preferred_element_type=F32)
    norms = jnp.sqrt(jnp.sum(merged * merged, axis=0))
    col_scale = (mag / norms).reshape(1, HD)
    cos, sin = rope_tables()
    cos_here = lax.dynamic_slice(cos, (zl * PAIR, 0), (PAIR, HD))
    sin_here = lax.dynamic_slice(sin, (zl * PAIR, 0), (PAIR, HD))
    rows = project(place, pair, w_key, w_val, far, down, ups, cos_here, sin_here)
    rows = lax.all_to_all(rows, "zl", 0, 0, tiled=True).reshape(SEQ, 3 * HD)
    grads, up_grad, mag_grad = attend(queries, grad_attn, rows, col_scale, all_down, cos, sin)
    grads = lax.all_to_all(grads.reshape(4, PAIR, 2 * HD), "zl", 0, 0, tiled=True)
    rank = rank_part(place, grads, ups)
    rank = (rank + lax.ppermute(rank, "core", swap)).astype(BF)
    mine, theirs = back(place, grads, w_key, w_val, far)
    theirs = lax.ppermute(theirs, "core", swap)
    small = jnp.concatenate([up_grad, mag_grad / norms], axis=0)
    small = lax.all_to_all(jnp.broadcast_to(small[None], (32, 40, HD)), DP, 0, 0, tiled=True)
    small = jnp.sum(small, axis=0)
    pieces = lax.all_to_all(down_part(place, rank, pair), DP + ("zl",), 0, 0, tiled=True)
    grad_down = jnp.sum(pieces, axis=0).reshape(8, 4, 32).transpose(1, 0, 2).reshape(RANK, 32)
    grad_hidden = join(place, rank, mine, theirs, factor)
    return grad_hidden, grad_down, small[:RANK], small[RANK]


def solution(mesh):
    fine = Mesh(np.asarray(mesh.devices).reshape(4, 4, 2, 4, 2), EVERY)
    tensor = ("zl", "core")
    return jax.shard_map(
        shards,
        mesh=fine,
        in_specs=(
            P(EVERY, None),
            P(None, tensor),
            P(None, tensor),
            P(),
            P(None, tensor),
            P(tensor),
            P(DP, tensor),
            P(DP, tensor),
        ),
        out_specs=(P(EVERY, None), P(None, EVERY), P(None, tensor), P(tensor)),
        check_vma=False,
    )
```

time: 1750 us -> 296 us (0.17)
  waiting for transfers between devices: 1400 us -> 143 us
  blocking collectives: 197 us -> 0 us
  matrix products: 91.8 us -> 4.23 us
  Pallas kernels: 0 us -> 47.3 us
  starting transfers between devices: 0.16 us -> 47.4 us
    unnamed x6 -> x1, waiting for transfers between devices: 1070 us -> 0.02 us
    psum x1 -> x0, blocking collectives: 197 us -> none  [shards(): right_sum, mag_sum = lax.psum((right_piece, mag_term), 'dp')]
    reduce_scatter x1 -> x0, waiting for transfers between devices: 170 us -> none  [shards(): lax.psum_scatter((jnp.einsum('th,dh->td', grad_key, w_key, preferred_elem...]
    dot_general x19 -> x2, matrix products: 91.8 us -> 4.23 us  [the longest x1 2.88 us: shards(): lax.dot_general(factor, up, TN, preferred_element_type=F32)]
    all_gather x1, waiting for transfers between devices: 161 us -> 78.5 us  [gather_weights(): lax.all_gather(jnp.concatenate([g[:512] for g in got], axis=1), ('x', 'y'...]
    pallas_call x0 -> x6, Pallas kernels: none -> 47.3 us  [the longest x1 15.3 us: back(): pl.pallas_call(back_kernel, grid=(D // KB,), in_specs=[smem(), whole((4,...]
    all_to_all x0 -> x5, waiting for transfers between devices: none -> 45 us  [the longest x1 17.1 us: shards(): lax.all_to_all(down_part(place, rank, pair), DP + ('zl',), 0, 0, tiled=True)]
    all_to_all x0 -> x5, starting transfers between devices: none -> 35.5 us  [the longest x1 13.7 us: shards(): lax.all_to_all(down_part(place, rank, pair), DP + ('zl',), 0, 0, tiled=True)]
  transfers between devices with their start and end apart: 4 -> 12, of which waited for: 4 -> 8; matrix products, arithmetic and copies ran while one was open for 3% -> 6% of each run, Pallas kernels for 0% -> 10%
where the time goes in v1:
time: 296 us; the launch traced here: 294 us
  waiting for transfers between devices  143 us (48%)
  starting transfers between devices  47.4 us (16%)
  Pallas kernels  47.3 us (16%)
  local copies, waits for them, and re-layouts  25.8 us (9%)
  between operations  14.3 us (5%)
  other arithmetic  12.2 us (4%)
  matrix products  4.23 us (1%)
    all_gather x1, waiting for transfers between devices, gather_weights(): lax.all_gather(jnp.concatenate([g[:512] for g in got], axis=1), ('x', 'y'...  78.5 us
    unnamed x38, local copies, waits for them, and re-layouts  21.1 us
    all_to_all x1, waiting for transfers between devices, shards(): lax.all_to_all(down_part(place, rank, pair), DP + ('zl',), 0, 0, tiled=True)  17.1 us
    ppermute x3, waiting for transfers between devices, gather_weights(): lax.ppermute(seed, ('zh', 'zl'), [(i, (i + shift) % 8) for i in range(8)])  15.3 us
    pallas_call x1, Pallas kernels, back(): pl.pallas_call(back_kernel, grid=(D // KB,), in_specs=[smem(), whole((4,...  15.3 us
    all_to_all x1, waiting for transfers between devices, shards(): rows = lax.all_to_all(rows, 'zl', 0, 0, tiled=True).reshape(SEQ, 3 * HD)  14 us
    all_to_all x1, waiting for transfers between devices, shards(): lax.all_to_all(grads.reshape(4, PAIR, 2 * HD), 'zl', 0, 0, tiled=True)  13.9 us
    all_to_all x1, starting transfers between devices, shards(): lax.all_to_all(down_part(place, rank, pair), DP + ('zl',), 0, 0, tiled=True)  13.7 us
  transfers between devices with their start and end apart: 12, of which 8 were waited for; matrix products, arithmetic and copies ran while one was open for 6% of the time, Pallas kernels for 10%

profile of v1, /device:TPU:1, one launch (start us, length us, event | category | flops | bytes accessed | tf_op | source)
XLA Modules:
  0.0 294.4 jit_solution(16156964981991545391)
XLA Ops:
  7.2 0.0 all-gather.2.cloned.1.call-start
  7.2 1.0 constant_dynamic-slice_fusion
  8.2 0.7 fusion.6
  9.0 6.5 %collective-permute-start.1 = (bf16[544,256]{1,0:T(8,128)(2,1)S(1)}, bf16[544,256]{1,0:T(8,128)(2,1)S(1)}, u32[]{:S(2)}, u32[]{:S(2)}) collective-permute-start(bf16[544,256]{1,0:T(8,128)(2,1)S(1)} %fusion.6), channel_id=1, source_target_pairs={{0,14},{2,0},{4,2},{6,4},{8,6},{10,8},{12,10},{14,12},{1,15},{3,1}... | collective-permute-start | bytes 835592 | tf_op jit(solution)/shard_map/ppermute | solution.py:304
  15.4 1.2 collective-permute-start.2
  16.6 0.7 collective-permute-start.3
  17.4 8.0 %collective-permute-done.1 = bf16[544,256]{1,0:T(8,128)(2,1)S(1)} collective-permute-done((bf16[544,256]{1,0:T(8,128)(2,1)S(1)}, bf16[544,256]{1,0:T(8,128)(2,1)S(1)}, u32[]{:S(2)}, u32[]{:S(2)}) %collective-permute-start.1) | collective-permute-done | bytes 278560 | tf_op jit(solution)/shard_map/ppermute | solution.py:304
  25.4 7.3 %collective-permute-done.2 = bf16[544,256]{1,0:T(8,128)(2,1)S(1)} collective-permute-done((bf16[544,256]{1,0:T(8,128)(2,1)S(1)}, bf16[544,256]{1,0:T(8,128)(2,1)S(1)}, u32[]{:S(2)}, u32[]{:S(2)}) %collective-permute-start.2) | collective-permute-done | bytes 278560 | tf_op jit(solution)/shard_map/ppermute | solution.py:304
  32.8 0.9 pad_maximum_fusion
  33.7 0.0 all-gather.2.cloned.1.call-update
  33.7 1.6 collective-permute-start
  35.4 0.1 pad_add_fusion.place
  35.4 2.0 fusion.4
  37.4 0.1 fusion.8
  37.6 0.6 copy-done.15
  38.2 0.2 copy-done.14
  38.4 0.0 copy-start.9
  38.4 1.1 collective-permute-done
  39.5 4.4 %maximum_select_fusion.hid = bf16[256,8192]{1,0:T(8,128)(2,1)S(1)} fusion(bf16[128,8192]{1,0:T(8,128)(2,1)} %collective-permute-done, bf16[128,8192]{1,0:T(8,128)(2,1)} %param.8, pred[]{:T(512)S(6)} %eq.3), kind=kLoop, calls=%fused_computation.3 | loop fusion | flops 18874368 | bytes 8388609 | tf_op jit(solution)/shard_map/jit(_where)/select_n | solution.py:316
  43.9 0.0 copy-start.4
  43.9 1.3 convolution_convert_fusion
  45.2 0.0 copy-start
  45.3 1.9 copy-done
  47.2 0.1 copy.24.down
  47.3 0.7 broadcast_in_dim.4
  48.0 3.6 %all-to-all-start.1 = ((bf16[4,256,32]{1,2,0:T(8,128)(2,1)}), bf16[4,256,32]{1,2,0:T(8,128)(2,1)S(1)}, u32[]{:S(2)}, u32[]{:S(2)}) async-start(bf16[4,256,32]{1,2,0:T(8,128)(2,1)} %broadcast_in_dim.4), calls=%async_computation.1 | async-start | bytes 131072 | tf_op jit(solution)/shard_map/all_to_all | solution.py:320
  51.6 78.5 %all-gather.2.cloned.1.call-done.far = bf16[8192,768]{1,0:T(8,128)(2,1)} async-done(((bf16[512,768]{1,0:T(8,128)(2,1)}), bf16[8192,768]{1,0:T(8,128)(2,1)}) %all-gather.2.cloned.1.call-update) | async-done | bytes 12582928 | tf_op jit(solution)/shard_map/all_gather | solution.py:305
  130.1 2.2 copy-done.1
  132.3 4.6 %copy-done.3 = bf16[8192,768]{1,0:T(8,128)(2,1)S(1)} copy-done((bf16[8192,768]{1,0:T(8,128)(2,1)S(1)}, bf16[8192,768]{1,0:T(8,128)(2,1)}, u32[]{:S(2)}) %copy-start.3) | copy-done | bytes 12582936
  136.9 1.6 copy-done.5
  138.5 9.6 %project.1 = bf16[4,256,384]{2,1,0:T(8,128)(2,1)} custom-call(s32[2]{0:T(128)S(1)} %pad_add_fusion.place, bf16[256,8192]{1,0:T(8,128)(2,1)S(1)} %copy-done.1, bf16[8192,128]{1,0:T(8,128)(2,1)S(1)} %copy-done.4, bf16[8192,128]{1,0:T(8,128)(2,1)S(1)} %copy-done.5, bf16[8192,768]{1,0:T(8,128)(2,1)S(1)} %copy-done.3, bf16[256,32]{1,0:T(8,128)(2,1)S(1)} %copy.24.down, ...), custom_call_target="tpu_custom_call" | custom-call | flops 4294967296 | bytes 20971520 | tf_op jit(solution)/shard_map/project/pallas_call | solution.py:82
  148.1 4.5 %all-to-all-start = ((bf16[4,256,384]{2,1,0:T(8,128)(2,1)}), bf16[4,256,384]{2,1,0:T(8,128)(2,1)}, u32[]{:S(2)}, u32[]{:S(2)}) async-start(bf16[4,256,384]{2,1,0:T(8,128)(2,1)} %project.1), calls=%async_computation | async-start | bytes 1572864 | tf_op jit(solution)/shard_map/all_to_all | solution.py:330
  152.6 2.6 pad_maximum_fusion.1
  155.3 2.9 fusion.2
  158.2 0.2 copy.25
  158.4 14.0 %all-to-all-done = bf16[4,256,384]{2,1,0:T(8,128)(2,1)} async-done(((bf16[4,256,384]{2,1,0:T(8,128)(2,1)}), bf16[4,256,384]{2,1,0:T(8,128)(2,1)}, u32[]{:S(2)}, u32[]{:S(2)}) %all-to-all-start) | async-done | bytes 786464 | tf_op jit(solution)/shard_map/all_to_all | solution.py:330
  172.4 1.0 copy-done.10
  173.4 1.2 copy-done.12
  174.6 1.2 copy-done.13
  175.9 13.5 %attend.1 = (bf16[1024,256]{1,0:T(8,128)(2,1)S(1)}, f32[32,128]{1,0:T(8,128)S(1)}, f32[8,128]{1,0:T(8,128)S(1)}) custom-call(bf16[1024,512]{1,0:T(8,128)(2,1)S(1)} %copy-done.12, bf16[1024,512]{1,0:T(8,128)(2,1)S(1)} %copy-done.13, bf16[1024,384]{1,0:T(8,128)(2,1)} %bitcast.6.rows, f32[1,128]{1,0:T(1,128)S(1)} %get-tuple-element.15.col_scale, ...), custom_call_target="tpu_custom_call" | custom-call | flops 5368709120 | bytes 6291456 | tf_op jit(solution)/shard_map/attend/pallas_call | solution.py:151
  189.4 0.0 copy-start.11
  189.4 0.8 copy-done.11
  190.2 3.5 %all-to-all-start.2 = ((bf16[4,256,256]{2,1,0:T(8,128)(2,1)}), bf16[4,256,256]{2,1,0:T(8,128)(2,1)S(1)}, u32[]{:S(2)}, u32[]{:S(2)}) async-start(bf16[4,256,256]{2,1,0:T(8,128)(2,1)} %bitcast.24), calls=%async_computation.2 | async-start | bytes 1048576 | tf_op jit(solution)/shard_map/all_to_all | solution.py:332
  193.7 13.9 %all-to-all-done.2.grads = bf16[4,256,256]{2,1,0:T(8,128)(2,1)S(1)} async-done(((bf16[4,256,256]{2,1,0:T(8,128)(2,1)}), bf16[4,256,256]{2,1,0:T(8,128)(2,1)S(1)}, u32[]{:S(2)}, u32[]{:S(2)}) %all-to-all-start.2) | async-done | bytes 524320 | tf_op jit(solution)/shard_map/all_to_all | solution.py:332
  207.6 0.9 broadcast_in_dim.5
  208.5 10.2 %all-to-all-start.4 = ((f32[32,40,128]{2,1,0:T(8,128)}), f32[32,40,128]{2,1,0:T(8,128)}, u32[]{:S(2)}, u32[]{:S(2)}) async-start(f32[32,40,128]{2,1,0:T(8,128)} %broadcast_in_dim.5), calls=%async_computation.4 | async-start | bytes 1310720 | tf_op jit(solution)/shard_map/all_to_all | solution.py:338
  218.8 1.6 copy-done.6
  220.3 15.3 %back.1 = (f32[128,8192]{1,0:T(8,128)S(1)}, bf16[128,8192]{1,0:T(8,128)(2,1)}) custom-call(s32[2]{0:T(128)S(1)} %pad_add_fusion.place, bf16[4,256,256]{2,1,0:T(8,128)(2,1)S(1)} %all-to-all-done.2.grads, bf16[8192,128]{1,0:T(8,128)(2,1)S(1)} %copy-done.4, bf16[8192,128]{1,0:T(8,128)(2,1)S(1)} %copy-done.6, bf16[8192,768]{1,0:T(8,128)(2,1)} %all-gather.2.cloned.1.call-done.far), custom_call_target="tpu_custom_call" | custom-call | flops 4294967296 | bytes 24117248 | tf_op jit(solution)/shard_map/back/pallas_call | solution.py:219
  235.6 2.0 copy-done.7
  237.6 1.7 collective-permute-start.5
  239.3 0.7 rank_part.1
  240.1 0.1 collective-permute-start.4
  240.2 3.1 %collective-permute-done.4 = f32[256,32]{1,0:T(8,128)S(1)} collective-permute-done((f32[256,32]{1,0:T(8,128)S(1)}, f32[256,32]{1,0:T(8,128)S(1)}, u32[]{:S(2)}, u32[]{:S(2)}) %collective-permute-start.4) | collective-permute-done | bytes 32800 | tf_op jit(solution)/shard_map/ppermute | solution.py:334
  243.3 4.9 %down_part.1 = f32[128,8,128]{2,1,0:T(8,128)} custom-call(s32[2]{0:T(128)S(1)} %pad_add_fusion.place, bf16[256,32]{1,0:T(8,128)(2,1)S(1)} %add_convert_fusion.rank, bf16[256,8192]{1,0:T(8,128)(2,1)S(1)} %copy-done.2), custom_call_target="tpu_custom_call" | custom-call | flops 134217728 | bytes 5242880 | tf_op jit(solution)/shard_map/down_part/pallas_call | solution.py:258
  248.2 13.7 %all-to-all-start.3 = ((f32[128,8,128]{2,1,0:T(8,128)}), f32[128,8,128]{2,1,0:T(8,128)S(1)}, u32[]{:S(2)}, u32[]{:S(2)}) async-start(f32[128,8,128]{2,1,0:T(8,128)} %down_part.1), calls=%async_computation.3 | async-start | bytes 1048576 | tf_op jit(solution)/shard_map/all_to_all | solution.py:340
  261.9 1.1 reduce_sum.29
  263.1 0.6 slice.38
  263.7 0.5 slice_bitcast_fusion.3
  264.2 17.1 %all-to-all-done.3 = f32[128,8,128]{2,1,0:T(8,128)S(1)} async-done(((f32[128,8,128]{2,1,0:T(8,128)}), f32[128,8,128]{2,1,0:T(8,128)S(1)}, u32[]{:S(2)}, u32[]{:S(2)}) %all-to-all-start.3) | async-done | bytes 524320 | tf_op jit(solution)/shard_map/all_to_all | solution.py:340
  281.3 0.1 reduce_sum.28
  281.4 0.1 reshape.41
  281.5 0.6 copy.28
  282.1 2.2 copy-done.8
  284.3 3.2 %join.1 = bf16[128,8192]{1,0:T(8,128)(2,1)} custom-call(s32[2]{0:T(128)S(1)} %pad_add_fusion.place, bf16[256,32]{1,0:T(8,128)(2,1)S(1)} %add_convert_fusion.rank, f32[128,8192]{1,0:T(8,128)S(1)} %copy-done.8, bf16[128,8192]{1,0:T(8,128)(2,1)S(1)} %collective-permute-done.5.theirs, bf16[32,8192]{1,0:T(8,128)(2,1)S(1)} %copy-done.9), custom_call_target="tpu_custom_call" | custom-call | flops 67108864 | bytes 9437184 | tf_op jit(solution)/shard_map/join/pallas_call | solution.py:278
  (37 shorter events, 0.2 us)
Async XLA Ops:
  7.2 123.0 %all-gather.2.cloned.1.call-start = ((), (), s32[]{:S(2)}) async-start(), calls=%async_computation.5 | async-start | bytes 13369344 | tf_op jit(solution)/shard_map/all_gather | solution.py:305
  7.2 31.2 %copy-start.17 = (bf16[32,128]{1,0:T(8,128)(2,1)S(1)}, bf16[32,128]{1,0:T(8,128)(2,1)}, u32[]{:S(2)}) copy-start(bf16[32,128]{1,0:T(8,128)(2,1)} %param.12) | copy-start | bytes 24580
  9.0 16.4 %collective-permute-start.1 = (bf16[544,256]{1,0:T(8,128)(2,1)S(1)}, bf16[544,256]{1,0:T(8,128)(2,1)S(1)}, u32[]{:S(2)}, u32[]{:S(2)}) collective-permute-start(bf16[544,256]{1,0:T(8,128)(2,1)S(1)} %fusion.6), channel_id=1, source_target_pairs={{0,14},{2,0},{4,2},{6,4},{8,6},{10,8},{12,10},{14,12},{1,15},{3,1}... | collective-permute-start | bytes 835592 | tf_op jit(solution)/shard_map/ppermute | solution.py:304
  15.4 17.3 %collective-permute-start.2 = (bf16[544,256]{1,0:T(8,128)(2,1)S(1)}, bf16[544,256]{1,0:T(8,128)(2,1)S(1)}, u32[]{:S(2)}, u32[]{:S(2)}) collective-permute-start(bf16[544,256]{1,0:T(8,128)(2,1)S(1)} %fusion.6), channel_id=1, source_target_pairs={{0,12},{2,14},{4,0},{6,2},{8,4},{10,6},{12,8},{14,10},{1,13},{3,15... | collective-permute-start | bytes 835592 | tf_op jit(solution)/shard_map/ppermute | solution.py:304
  16.6 16.1 %collective-permute-start.3 = (bf16[544,256]{1,0:T(8,128)(2,1)S(1)}, bf16[544,256]{1,0:T(8,128)(2,1)S(1)}, u32[]{:S(2)}, u32[]{:S(2)}) collective-permute-start(bf16[544,256]{1,0:T(8,128)(2,1)S(1)} %fusion.6), channel_id=1, source_target_pairs={{0,2},{2,4},{4,6},{6,8},{8,10},{10,12},{12,14},{14,0},{1,3},{3,5},... | collective-permute-start | bytes 835592 | tf_op jit(solution)/shard_map/ppermute | solution.py:304
  33.7 5.8 %collective-permute-start = (bf16[128,8192]{1,0:T(8,128)(2,1)}, bf16[128,8192]{1,0:T(8,128)(2,1)}, u32[]{:S(2)}, u32[]{:S(2)}) collective-permute-start(bf16[128,8192]{1,0:T(8,128)(2,1)} %param.8), channel_id=1, source_target_pairs={{0,1},{1,0},{2,3},{3,2},{4,5},{5,4},{6,7},{7,6},{8,9},{9,8},{10,11... | collective-permute-start | bytes 6291464 | tf_op jit(solution)/shard_map/ppermute | solution.py:315
  37.4 0.8 copy-start.15
  37.4 1.0 copy-start.14
  37.4 2.1 copy-start.16
  38.4 5.5 %copy-start.9 = (bf16[32,8192]{1,0:T(8,128)(2,1)S(1)}, bf16[32,8192]{1,0:T(8,128)(2,1)}, u32[]{:S(2)}) copy-start(bf16[32,8192]{1,0:T(8,128)(2,1)} %factor.1) | copy-start | bytes 1572868
  43.9 86.3 %copy-start.4 = (bf16[8192,128]{1,0:T(8,128)(2,1)S(1)}, bf16[8192,128]{1,0:T(8,128)(2,1)}, u32[]{:S(2)}) copy-start(bf16[8192,128]{1,0:T(8,128)(2,1)} %own_key.3) | copy-start | bytes 6291460
  45.2 1.9 copy-start
  48.0 100.1 %all-to-all-start.1 = ((bf16[4,256,32]{1,2,0:T(8,128)(2,1)}), bf16[4,256,32]{1,2,0:T(8,128)(2,1)S(1)}, u32[]{:S(2)}, u32[]{:S(2)}) async-start(bf16[4,256,32]{1,2,0:T(8,128)(2,1)} %broadcast_in_dim.4), calls=%async_computation.1 | async-start | bytes 131072 | tf_op jit(solution)/shard_map/all_to_all | solution.py:320
  130.1 2.2 copy-start.1
  132.3 4.6 %copy-start.3 = (bf16[8192,768]{1,0:T(8,128)(2,1)S(1)}, bf16[8192,768]{1,0:T(8,128)(2,1)}, u32[]{:S(2)}) copy-start(bf16[8192,768]{1,0:T(8,128)(2,1)} %all-gather.2.cloned.1.call-done.far) | copy-start | bytes 37748740
  136.9 1.6 copy-start.5
  148.1 24.2 %all-to-all-start = ((bf16[4,256,384]{2,1,0:T(8,128)(2,1)}), bf16[4,256,384]{2,1,0:T(8,128)(2,1)}, u32[]{:S(2)}, u32[]{:S(2)}) async-start(bf16[4,256,384]{2,1,0:T(8,128)(2,1)} %project.1), calls=%async_computation | async-start | bytes 1572864 | tf_op jit(solution)/shard_map/all_to_all | solution.py:330
  152.6 5.5 %copy-start.18 = (f32[128]{0:T(128)S(1)}, f32[128]{0:T(128)}, u32[]{:S(2)}) copy-start(f32[128]{0:T(128)} %param.13) | copy-start | bytes 1540
  172.4 1.0 copy-start.10
  173.4 1.2 copy-start.12
  174.6 1.2 copy-start.13
  189.4 0.8 copy-start.11
  190.2 17.4 %all-to-all-start.2 = ((bf16[4,256,256]{2,1,0:T(8,128)(2,1)}), bf16[4,256,256]{2,1,0:T(8,128)(2,1)S(1)}, u32[]{:S(2)}, u32[]{:S(2)}) async-start(bf16[4,256,256]{2,1,0:T(8,128)(2,1)} %bitcast.24), calls=%async_computation.2 | async-start | bytes 1048576 | tf_op jit(solution)/shard_map/all_to_all | solution.py:332
  208.5 39.7 %all-to-all-start.4 = ((f32[32,40,128]{2,1,0:T(8,128)}), f32[32,40,128]{2,1,0:T(8,128)}, u32[]{:S(2)}, u32[]{:S(2)}) async-start(f32[32,40,128]{2,1,0:T(8,128)} %broadcast_in_dim.5), calls=%async_computation.4 | async-start | bytes 1310720 | tf_op jit(solution)/shard_map/all_to_all | solution.py:338
  218.7 1.6 copy-start.6
  220.3 23.0 %copy-start.2 = (bf16[256,8192]{1,0:T(8,128)(2,1)S(1)}, bf16[256,8192]{1,0:T(8,128)(2,1)}, u32[]{:S(2)}) copy-start(bf16[256,8192]{1,0:T(8,128)(2,1)} %copy-done) | copy-start | bytes 12582916
  235.6 2.0 copy-start.7
  237.6 44.5 %collective-permute-start.5 = (bf16[128,8192]{1,0:T(8,128)(2,1)}, bf16[128,8192]{1,0:T(8,128)(2,1)S(1)}, u32[]{:S(2)}, u32[]{:S(2)}) collective-permute-start(bf16[128,8192]{1,0:T(8,128)(2,1)} %get-tuple-element.11), channel_id=1, source_target_pairs={{0,1},{1,0},{2,3},{3,2},{4,5},{5,4},{6,7},{7,6},{8,9},{9,8},{10,11... | collective-permute-start | bytes 6291464 | tf_op jit(solution)/shard_map/ppermute | solution.py:336
  240.1 3.2 %collective-permute-start.4 = (f32[256,32]{1,0:T(8,128)S(1)}, f32[256,32]{1,0:T(8,128)S(1)}, u32[]{:S(2)}, u32[]{:S(2)}) collective-permute-start(f32[256,32]{1,0:T(8,128)S(1)} %rank_part.1), channel_id=1, source_target_pairs={{0,1},{1,0},{2,3},{3,2},{4,5},{5,4},{6,7},{7,6},{8,9},{9,8},{10,11... | collective-permute-start | bytes 98312 | tf_op jit(solution)/shard_map/ppermute | solution.py:334
  248.2 33.0 %all-to-all-start.3 = ((f32[128,8,128]{2,1,0:T(8,128)}), f32[128,8,128]{2,1,0:T(8,128)S(1)}, u32[]{:S(2)}, u32[]{:S(2)}) async-start(f32[128,8,128]{2,1,0:T(8,128)} %down_part.1), calls=%async_computation.3 | async-start | bytes 1048576 | tf_op jit(solution)/shard_map/all_to_all | solution.py:340
  282.1 2.2 copy-start.8
Sparse Core Ops, SparseCore 0:
  33.8 96.2 all-gather.1

commit v2 on v1

v2 whole, which is shorter than its diff:
```python
import jax
import jax.numpy as jnp
import numpy as np
from jax import lax
from jax.experimental import pallas as pl
from jax.experimental.pallas import tpu as pltpu
from jax.sharding import Mesh, PartitionSpec as P

HD = 128
D = 8192
SEQ = 1024
RANK = 32
PAIR = 256
NEAR = 4096
CROSS = 2048
LINE = 2048
CHUNK = 1024
QB = 256
GROUP = 4
SCALE = 2.0
ROPE_BASE = 500000.0
LOG2E = 1.4426950408889634
INV_SQRT = HD ** (-0.5)
MIB = 1024 * 1024
BF = jnp.bfloat16
F32 = jnp.float32
NT = (((1,), (1,)), ((), ()))
TN = (((0,), (0,)), ((), ()))
EVERY = ("x", "y", "zh", "zl", "core")
DP = ("x", "y", "zh")


def rope_tables():
    half = HD // 2
    frequency = ROPE_BASE ** (-(jnp.arange(half, dtype=F32) * 2.0 / HD))
    angles = jnp.arange(SEQ, dtype=F32)[:, None] * frequency[None, :]
    cosine, sine = jnp.cos(angles), jnp.sin(angles)
    return jnp.concatenate([cosine, cosine], 1), jnp.concatenate([-sine, sine], 1)


def smem():
    return pl.BlockSpec(memory_space=pltpu.SMEM)


def whole(shape):
    return pl.BlockSpec(shape, lambda *_: (0,) * len(shape))


def params(limit):
    return pltpu.CompilerParams(vmem_limit_bytes=limit * MIB)


def cost(flops, moved, trans=0):
    return pl.CostEstimate(flops=flops, bytes_accessed=moved, transcendentals=trans)


def any_ref():
    return pl.BlockSpec(memory_space=pl.ANY)


def start_all(copies):
    for copy in copies:
        copy.start()
    return copies


def wait_all(copies):
    for copy in copies:
        copy.wait()


def near_copies(base, own_key, own_val, far, weights, sems):
    chunks = []
    for i in range(far.shape[0] // CHUNK):
        here = pl.ds(i * CHUNK, CHUNK)
        there = pl.ds(base + i * CHUNK, CHUNK)
        chunks.append(
            [
                pltpu.make_async_copy(own_key.at[there, :], weights.at[here, pl.ds(0, HD)], sems.at[0, i]),
                pltpu.make_async_copy(own_val.at[there, :], weights.at[here, pl.ds(HD, HD)], sems.at[1, i]),
                pltpu.make_async_copy(far.at[here, :], weights.at[here, pl.ds(256, 768)], sems.at[2, i]),
            ]
        )
    return chunks


def line_copies(base, first, own_key, own_val, one, two_a, two_b, three, weights, sems):
    chunks = []
    size = LINE // 2
    for i, two in enumerate((two_a.at[pl.ds(RANK, size), :], two_b)):
        here = pl.ds(first + i * size, size)
        there = pl.ds(base + i * size, size)
        near = pl.ds(RANK + i * size, size)
        chunks.append(
            [
                pltpu.make_async_copy(own_key.at[there, :], weights.at[here, pl.ds(0, HD)], sems.at[0, i]),
                pltpu.make_async_copy(own_val.at[there, :], weights.at[here, pl.ds(HD, HD)], sems.at[1, i]),
                pltpu.make_async_copy(one.at[near, :], weights.at[here, pl.ds(256, 256)], sems.at[2, i]),
                pltpu.make_async_copy(two, weights.at[here, pl.ds(512, 256)], sems.at[3, i]),
                pltpu.make_async_copy(three.at[near, :], weights.at[here, pl.ds(768, 256)], sems.at[4, i]),
            ]
        )
    return chunks


def pair_copies(pair, hid, base, count, sem):
    size = hid.shape[1] // count
    return [
        pltpu.make_async_copy(
            pair.at[:, pl.ds(base + i * size, size)], hid.at[:, pl.ds(i * size, size)], sem.at[i]
        )
        for i in range(count)
    ]


def multiply(acc, chunks, hid_chunks, hid, weights):
    size = hid.shape[1] // len(chunks)
    for i, chunk in enumerate(chunks):
        wait_all(chunk + [hid_chunks[i]])
        here = slice(i * size, (i + 1) * size)
        term = jnp.dot(hid[:, here], weights[here, :], preferred_element_type=F32)
        acc = term if acc is None else acc + term
    return acc


def project_line_kernel(
    pair, own_key, own_val, cross, one, two_a, two_b, three, out, hid, weights, hid_sem, sems, line_sems
):
    chunks = near_copies(NEAR, own_key, own_val, cross, weights, sems)
    chunks += line_copies(
        NEAR + CROSS, CROSS, own_key, own_val, one, two_a, two_b, three, weights, line_sems
    )
    hid_chunks = pair_copies(pair, hid, NEAR, 4, hid_sem)
    for i in range(4):
        start_all(chunks[i] + [hid_chunks[i]])
    out[...] = multiply(None, chunks, hid_chunks, hid, weights)


def project_line(pair, w_key, w_val, cross, line):
    return pl.pallas_call(
        project_line_kernel,
        in_specs=[any_ref()] * 8,
        out_specs=whole((PAIR, 1024)),
        out_shape=jax.ShapeDtypeStruct((PAIR, 1024), F32),
        scratch_shapes=[
            pltpu.VMEM((PAIR, CROSS + LINE), BF),
            pltpu.VMEM((CROSS + LINE, 1024), BF),
            pltpu.SemaphoreType.DMA((4,)),
            pltpu.SemaphoreType.DMA((3, 2)),
            pltpu.SemaphoreType.DMA((5, 2)),
        ],
        compiler_params=params(60),
        cost_estimate=cost(2 * PAIR * (CROSS + LINE) * 1024, 11 * MIB),
        name="project_line",
    )(pair, w_key, w_val, cross, *line)


def project_kernel(
    place, pair, own_key, own_val, far, so_far, down, ups, cos, sin, out, hid, weights, hid_sem, sems
):
    count = NEAR // CHUNK
    chunks = near_copies(0, own_key, own_val, far, weights, sems)
    hid_chunks = pair_copies(pair, hid, 0, count, hid_sem)
    for i in range(count):
        start_all(chunks[i] + [hid_chunks[i]])
    acc = multiply(so_far[...], chunks, hid_chunks, hid, weights)
    for r in range(4):
        key = acc[:, r * 256 : r * 256 + HD]
        turned = key * cos[...] + pltpu.roll(key, HD // 2, 1) * sin[...]
        turned = turned * (INV_SQRT * LOG2E)
        high = turned.astype(BF)
        low = (turned - high.astype(F32)).astype(BF)
        lifted = jnp.dot(down[...], ups[r], preferred_element_type=F32)
        base = (acc[:, r * 256 + HD : (r + 1) * 256] + SCALE * lifted).astype(BF)
        slot = lax.rem(place[0] + r, 4)
        out[slot] = jnp.concatenate([high, low, base], axis=1)


def project(place, pair, w_key, w_val, far, so_far, down, ups, cos, sin):
    count = NEAR // CHUNK
    return pl.pallas_call(
        project_kernel,
        in_specs=[
            smem(),
            any_ref(),
            any_ref(),
            any_ref(),
            any_ref(),
            whole((PAIR, 1024)),
            whole((PAIR, RANK)),
            whole((4, RANK, HD)),
            whole((PAIR, HD)),
            whole((PAIR, HD)),
        ],
        out_specs=whole((4, PAIR, 3 * HD)),
        out_shape=jax.ShapeDtypeStruct((4, PAIR, 3 * HD), BF),
        scratch_shapes=[
            pltpu.VMEM((PAIR, NEAR), BF),
            pltpu.VMEM((NEAR, 1024), BF),
            pltpu.SemaphoreType.DMA((count,)),
            pltpu.SemaphoreType.DMA((3, count)),
        ],
        compiler_params=params(60),
        cost_estimate=cost(2 * PAIR * NEAR * 1024, 14 * MIB),
        name="project",
    )(place, pair, w_key, w_val, far, so_far, down, ups, cos, sin)


def attend_kernel(query, grad, rows, col_scale, down, cos, sin, grads, up_grad, mag_grad, vals, dkey, dval):
    head = pl.program_id(0)

    @pl.when(head == 0)
    def _():
        vals[...] = (rows[:, 2 * HD :].astype(F32) * col_scale[...]).astype(BF)
        dkey[...] = jnp.zeros_like(dkey)
        dval[...] = jnp.zeros_like(dval)

    for block in range(SEQ // QB):
        stop = (block + 1) * QB
        here = slice(block * QB, stop)
        q = query[here, :]
        g = grad[here, :]
        qq = jnp.concatenate([q, q], axis=1)
        scores = lax.dot_general(rows[:stop, : 2 * HD], qq, NT, preferred_element_type=F32)
        key_at = lax.broadcasted_iota(jnp.int32, (QB, QB), 0)
        query_at = lax.broadcasted_iota(jnp.int32, (QB, QB), 1)
        edge = jnp.where(key_at <= query_at, scores[block * QB :], -1e30)
        if block:
            scores = jnp.concatenate([scores[: block * QB], edge], axis=0)
        else:
            scores = edge
        powers = jnp.exp2(scores - jnp.max(scores, axis=0, keepdims=True))
        attn = powers * (1.0 / jnp.sum(powers, axis=0, keepdims=True))
        half = attn.astype(BF)
        pgrad = lax.dot_general(vals[:stop], g, NT, preferred_element_type=F32)
        delta = jnp.sum(half.astype(F32) * pgrad, axis=0, keepdims=True)
        sgrad = (attn * (pgrad - delta)).astype(BF)
        dval[:stop] += jnp.dot(half, g, preferred_element_type=F32)
        dkey[:stop] += jnp.dot(sgrad, q, preferred_element_type=F32)

    @pl.when(head == pl.num_programs(0) - 1)
    def _():
        dk = dkey[...] * INV_SQRT
        dk = dk * cos[...] - pltpu.roll(dk, HD // 2, 1) * sin[...]
        dv = dval[...]
        gv = (dv * col_scale[...]).astype(BF)
        grads[:, :HD] = dk.astype(BF)
        grads[:, HD:] = gv
        up_grad[...] = SCALE * lax.dot_general(down[...], gv, TN, preferred_element_type=F32)
        total = jnp.sum(dv * rows[:, 2 * HD :].astype(F32), axis=0, keepdims=True)
        mag_grad[...] = jnp.broadcast_to(total, mag_grad.shape)


def attend(queries, grad_attn, rows, col_scale, down, cos, sin):
    return pl.pallas_call(
        attend_kernel,
        grid=(GROUP,),
        in_specs=[
            pl.BlockSpec((SEQ, HD), lambda h: (0, h)),
            pl.BlockSpec((SEQ, HD), lambda h: (0, h)),
            whole((SEQ, 3 * HD)),
            whole((1, HD)),
            whole((SEQ, RANK)),
            whole((SEQ, HD)),
            whole((SEQ, HD)),
        ],
        out_specs=[whole((SEQ, 2 * HD)), whole((RANK, HD)), whole((8, HD))],
        out_shape=[
            jax.ShapeDtypeStruct((SEQ, 2 * HD), BF),
            jax.ShapeDtypeStruct((RANK, HD), F32),
            jax.ShapeDtypeStruct((8, HD), F32),
        ],
        scratch_shapes=[
            pltpu.VMEM((SEQ, HD), BF),
            pltpu.VMEM((SEQ, HD), F32),
            pltpu.VMEM((SEQ, HD), F32),
        ],
        compiler_params=params(60),
        cost_estimate=cost(5 * 2 * GROUP * SEQ * SEQ * HD, 6 * MIB, GROUP * SEQ * SEQ),
        name="attend",
    )(queries, grad_attn, rows, col_scale, down, cos, sin)


def rank_kernel(place, grads, ups, out):
    total = jnp.zeros((PAIR, RANK), F32)
    for r in range(4):
        slot = lax.rem(place[0] + r, 4)
        total += lax.dot_general(grads[slot, :, HD:], ups[r], NT, preferred_element_type=F32)
    out[...] = total


def rank_part(place, grads, ups):
    return pl.pallas_call(
        rank_kernel,
        in_specs=[smem(), whole((4, PAIR, 2 * HD)), whole((4, RANK, HD))],
        out_specs=whole((PAIR, RANK)),
        out_shape=jax.ShapeDtypeStruct((PAIR, RANK), F32),
        compiler_params=params(60),
        cost_estimate=cost(2 * PAIR * 512 * RANK, MIB),
        name="rank_part",
    )(place, grads, ups)


def spread(place, grads, left):
    first = pl.multiple_of(place[1] * 128, 128)
    second = pl.multiple_of(128 - place[1] * 128, 128)
    for r in range(4):
        slot = lax.rem(place[0] + r, 4)
        left[:128, r * 256 : (r + 1) * 256] = grads[slot, pl.ds(first, 128), :]
        left[128:, r * 256 : (r + 1) * 256] = grads[slot, pl.ds(second, 128), :]


def back_chunks(chunks, left, weights, mine, theirs, part, out_sem):
    size = weights.shape[0] // len(chunks)
    leaving = []
    for i, chunk in enumerate(chunks):
        wait_all(chunk)
        here = slice(i * size, (i + 1) * size)
        part[:, here] = lax.dot_general(left[...], weights[here, :], NT, preferred_element_type=F32).astype(BF)
        cols = pl.ds(i * size, size)
        leaving += start_all(
            [
                pltpu.make_async_copy(part.at[pl.ds(0, 128), cols], mine.at[:, cols], out_sem.at[0, i]),
                pltpu.make_async_copy(part.at[pl.ds(128, 128), cols], theirs.at[:, cols], out_sem.at[1, i]),
            ]
        )
    wait_all(leaving)


def back_line_kernel(
    place, grads, own_key, own_val, cross, one, two_a, two_b, three, _, mine, theirs, left, weights, part, out_sem, sems,
    line_sems,
):
    chunks = near_copies(NEAR, own_key, own_val, cross, weights, sems)
    chunks += line_copies(
        NEAR + CROSS, CROSS, own_key, own_val, one, two_a, two_b, three, weights, line_sems
    )
    for chunk in chunks:
        start_all(chunk)
    spread(place, grads, left)
    back_chunks(chunks, left, weights, mine, theirs, part, out_sem)


def back_near_kernel(place, grads, own_key, own_val, far, _, mine, theirs, left, weights, part, out_sem, sems):
    chunks = near_copies(0, own_key, own_val, far, weights, sems)
    for chunk in chunks:
        start_all(chunk)
    spread(place, grads, left)
    back_chunks(chunks, left, weights, mine, theirs, part, out_sem)


def back(kernel, kinds, name, place, grads, w_key, w_val, others, after):
    rows = D // 2
    count = rows // CHUNK
    return pl.pallas_call(
        kernel,
        in_specs=[smem(), whole((4, PAIR, 2 * HD))] + [any_ref()] * (3 + len(others)),
        out_specs=[any_ref()] * 2,
        out_shape=[jax.ShapeDtypeStruct((128, rows), BF)] * 2,
        scratch_shapes=[
            pltpu.VMEM((PAIR, 1024), BF),
            pltpu.VMEM((rows, 1024), BF),
            pltpu.VMEM((PAIR, rows), BF),
            pltpu.SemaphoreType.DMA((2, count)),
        ]
        + [pltpu.SemaphoreType.DMA(kind) for kind in kinds],
        compiler_params=params(60),
        cost_estimate=cost(MIB, MIB),
        name=name,
    )(place, grads, w_key, w_val, *others, after)


def down_kernel(place, rank, hid, out):
    part = SCALE * lax.dot_general(rank[...], hid[...], TN, preferred_element_type=F32)
    lane = lax.broadcasted_iota(jnp.int32, (8, HD), 1) // 32
    core = place[1]
    for tile in range(part.shape[1] // HD):
        regs = [part[8 * i : 8 * i + 8, tile * HD : (tile + 1) * HD] for i in range(4)]
        blocks = []
        for pick in range(2):
            column = 2 * pick + core
            block = jnp.zeros((8, HD), F32)
            for i in range(4):
                moved = pltpu.roll(regs[i], lax.rem((i - column + 4) * 32, HD), 1)
                block = jnp.where(lane == i, moved, block)
            blocks.append(block)
        out[16 * tile : 16 * tile + 16, :] = jnp.concatenate(blocks, axis=0).astype(BF)


def down_part(place, rank, pair):
    wide = 2048
    return pl.pallas_call(
        down_kernel,
        grid=(D // wide,),
        in_specs=[smem(), whole((PAIR, RANK)), pl.BlockSpec((PAIR, wide), lambda k: (0, k))],
        out_specs=pl.BlockSpec((wide // 8, HD), lambda k: (k, 0)),
        out_shape=jax.ShapeDtypeStruct((1024, HD), BF),
        compiler_params=params(60),
        cost_estimate=cost(2 * PAIR * D * RANK, 5 * MIB),
        name="down_part",
    )(place, rank, pair)


def finish_kernel(pieces, _, out):
    total = jnp.sum(pieces[...].astype(F32).reshape(128, 8, HD), axis=0)
    for i in range(4):
        out[8 * i : 8 * i + 8, :] = total[:, 32 * i : 32 * i + 32]


def finish(pieces, after):
    return pl.pallas_call(
        finish_kernel,
        in_specs=[whole((1024, HD)), any_ref()],
        out_specs=whole((RANK, 32)),
        out_shape=jax.ShapeDtypeStruct((RANK, 32), F32),
        compiler_params=params(60),
        cost_estimate=cost(MIB, MIB),
        name="finish",
    )(pieces, after)


def join_kernel(place, rank, mine_a, theirs_a, mine_b, theirs_b, factor, out, one, two, result, sems, out_sem):
    half = D // 2
    count = half // CHUNK
    chunks = []
    for i in range(2 * count):
        own, other = (mine_a, theirs_a) if i < count else (mine_b, theirs_b)
        here = pl.ds(i * CHUNK, CHUNK)
        there = pl.ds(i % count * CHUNK, CHUNK)
        chunks.append(
            start_all(
                [
                    pltpu.make_async_copy(own.at[:, there], one.at[:, here], sems.at[0, i]),
                    pltpu.make_async_copy(other.at[:, there], two.at[:, here], sems.at[1, i]),
                ]
            )
        )
    mine = rank[pl.ds(pl.multiple_of(place[1] * 128, 128), 128), :]
    leaving = []
    for i, chunk in enumerate(chunks):
        here = slice(i * CHUNK, (i + 1) * CHUNK)
        adapter = SCALE * jnp.dot(mine, factor[:, here], preferred_element_type=F32)
        wait_all(chunk)
        result[:, here] = (one[:, here].astype(F32) + two[:, here].astype(F32) + adapter).astype(BF)
        cols = pl.ds(i * CHUNK, CHUNK)
        leaving += start_all([pltpu.make_async_copy(result.at[:, cols], out.at[:, cols], out_sem.at[i])])
    wait_all(leaving)


def join(place, rank, mine_a, theirs_a, mine_b, theirs_b, factor):
    return pl.pallas_call(
        join_kernel,
        in_specs=[smem(), whole((PAIR, RANK))] + [any_ref()] * 4 + [whole((RANK, D))],
        out_specs=any_ref(),
        out_shape=jax.ShapeDtypeStruct((128, D), BF),
        scratch_shapes=[pltpu.VMEM((128, D), BF)] * 3
        + [pltpu.SemaphoreType.DMA((2, D // CHUNK)), pltpu.SemaphoreType.DMA((D // CHUNK,))],
        compiler_params=params(60),
        cost_estimate=cost(MIB, MIB),
        name="join",
    )(place, rank, mine_a, theirs_a, mine_b, theirs_b, factor)


def along_z(value, shift):
    return lax.ppermute(value, ("zh", "zl"), [(i, (i + shift) % 8) for i in range(8)])


def to_all(value, axis):
    return lax.all_to_all(jnp.broadcast_to(value[None], (4,) + value.shape), axis, 0, 0, tiled=True)


def gather_weights(w_key, w_val, up):
    place = lax.axis_index("x") * 4 + lax.axis_index("y")
    near, cross = NEAR // 16, CROSS // 16

    def rows(start, count):
        return [lax.dynamic_slice(w, (start, 0), (count, HD)) for w in (w_key, w_val)]

    seed = jnp.concatenate(
        [jnp.concatenate(rows(place * near, near), 1), jnp.concatenate(rows(NEAR + place * cross, cross), 1)], 0
    )
    half = (near + cross) // 2
    first = along_z(seed, -1)
    third = along_z(seed, 1)
    second = jnp.concatenate([along_z(seed[:half], -2), along_z(seed[half:], 2)], axis=0)
    seeds = jnp.concatenate([first, second, third], axis=1)
    far = lax.all_gather(seeds[:near], ("x", "y"), axis=0, tiled=True)
    cross_rows = to_all(to_all(seeds[near:], "y").reshape(4 * cross, 768), "x").reshape(CROSS, 768)
    base = NEAR + CROSS
    own = jnp.concatenate([w_key[base:], w_val[base:]], axis=1)
    own = jnp.concatenate([jnp.pad(up, ((0, 0), (0, HD))), own], axis=0) + seeds[:1, :1] * 0
    one = along_z(own, -1)
    three = along_z(own, 1)
    two_a = along_z(one[: RANK + LINE // 2], -1)
    two_b = along_z(three[RANK + LINE // 2 :], 1)
    ups = jnp.stack([up] + [got[:RANK, :HD] for got in (one, two_a, three)])
    return far, cross_rows, (one, two_a, two_b, three), ups


def shards(hidden, w_key, w_val, factor, up, mag, queries, grad_attn):
    zl, core = lax.axis_index("zl"), lax.axis_index("core")
    place = jnp.stack([zl, core]).astype(jnp.int32)
    swap = [(0, 1), (1, 0)]
    far, cross, line, ups = gather_weights(w_key, w_val, up)
    other = lax.ppermute(hidden, "core", swap)
    pair = jnp.where(
        core == 0, jnp.concatenate([hidden, other], axis=0), jnp.concatenate([other, hidden], axis=0)
    )
    down = lax.dot_general(pair, factor, NT, preferred_element_type=F32).astype(BF)
    all_down = lax.all_to_all(
        jnp.broadcast_to(down[None], (4, PAIR, RANK)), "zl", 0, 0, tiled=True
    ).reshape(SEQ, RANK)
    merged = w_val.astype(F32) + SCALE * lax.dot_general(factor, up, TN, preferred_element_type=F32)
    norms = jnp.sqrt(jnp.sum(merged * merged, axis=0))
    col_scale = (mag / norms).reshape(1, HD)
    cos, sin = rope_tables()
    cos_here = lax.dynamic_slice(cos, (zl * PAIR, 0), (PAIR, HD))
    sin_here = lax.dynamic_slice(sin, (zl * PAIR, 0), (PAIR, HD))
    so_far = project_line(pair, w_key, w_val, cross, line)
    rows = project(place, pair, w_key, w_val, far, so_far, down, ups, cos_here, sin_here)
    rows = lax.all_to_all(rows, "zl", 0, 0, tiled=True).reshape(SEQ, 3 * HD)
    grads, up_grad, mag_grad = attend(queries, grad_attn, rows, col_scale, all_down, cos, sin)
    grads = lax.all_to_all(grads.reshape(4, PAIR, 2 * HD), "zl", 0, 0, tiled=True)
    small = jnp.concatenate([up_grad, mag_grad / norms], axis=0)
    small = small + lax.ppermute(small, "zh", swap)
    small = lax.all_gather(jnp.pad(small, ((0, 88), (0, 0))), ("x", "y"), axis=0, tiled=True)
    small = jnp.sum(small.reshape(16, HD, HD)[:, :40], axis=0)
    part = rank_part(place, grads, ups)
    rank = (part + lax.ppermute(part, "core", swap)).astype(BF)
    pieces = down_part(place, rank, pair)
    mine_a, theirs_a = back(back_near_kernel, [(3, 4)], "back_near", place, grads, w_key, w_val, (far,), pieces)
    theirs_a = lax.ppermute(theirs_a, "core", swap)
    mine_b, theirs_b = back(
        back_line_kernel, [(3, 2), (5, 2)], "back_line", place, grads, w_key, w_val, (cross,) + line, pieces
    )
    theirs_b = lax.ppermute(theirs_b, "core", swap)
    pieces = lax.all_to_all(pieces, DP + ("zl",), 0, 0, tiled=True)
    grad_hidden = join(place, rank, mine_a, theirs_a, mine_b, theirs_b, factor)
    grad_down = finish(pieces, grad_hidden)
    return grad_hidden, grad_down, small[:RANK], small[RANK]


def solution(mesh):
    fine = Mesh(np.asarray(mesh.devices).reshape(4, 4, 2, 4, 2), EVERY)
    tensor = ("zl", "core")
    return jax.shard_map(
        shards,
        mesh=fine,
        in_specs=(
            P(EVERY, None),
            P(None, tensor),
            P(None, tensor),
            P(),
            P(None, tensor),
            P(tensor),
            P(DP, tensor),
            P(DP, tensor),
        ),
        out_specs=(P(EVERY, None), P(None, EVERY), P(None, tensor), P(tensor)),
        check_vma=False,
    )
```

time: 296 us -> 261 us (0.88)
  waiting for transfers between devices: 143 us -> 96.8 us
  Pallas kernels: 47.3 us -> 55.9 us
  other arithmetic: 12.2 us -> 19.9 us
  local copies, waits for them, and re-layouts: 25.8 us -> 19.5 us
    all_gather x1 -> x2, waiting for transfers between devices: 78.5 us -> 0.02 us  [the longest x1 0.02 us: gather_weights(): far = lax.all_gather(seeds[:near], ('x', 'y'), axis=0, tiled=True)]
    all_to_all x2 -> x3, waiting for transfers between devices: 17.1 us -> 57.6 us  [the longest x2 50.2 us: to_all(): lax.all_to_all(jnp.broadcast_to(value[None], (4,) + value.shape), axis, 0...]
    unnamed x38 -> x28, local copies, waits for them, and re-layouts: 21.1 us -> 5.09 us
    pallas_call x3 -> x6, Pallas kernels: 28.1 us -> 34.7 us  [the longest x2 13.3 us: back(): pl.pallas_call(kernel, in_specs=[smem(), whole((4, PAIR, 2 * HD))] + [any...]
    ppermute x5 -> x12, starting transfers between devices: 10.2 us -> 16.6 us  [the longest x8 14.4 us: along_z(): lax.ppermute(value, ('zh', 'zl'), [(i, (i + shift) % 8) for i in range(8)])]
    all_to_all x2 -> x3, starting transfers between devices: 23.9 us -> 18 us  [the longest x1 9.88 us: shards(): pieces = lax.all_to_all(pieces, DP + ('zl',), 0, 0, tiled=True)]
    slice x3 -> x9, local copies, waits for them, and re-layouts: 0.05 us -> 4.43 us  [the longest x1 2.02 us: gather_weights(): two_b = along_z(three[RANK + LINE // 2:], 1)]
    all_to_all x1, waiting for transfers between devices: 13.9 us -> 9.64 us  [shards(): lax.all_to_all(grads.reshape(4, PAIR, 2 * HD), 'zl', 0, 0, tiled=True)]
  transfers between devices with their start and end apart: 12 -> 21, of which waited for: 8 -> 9; matrix products, arithmetic and copies ran while one was open for 6% -> 12% of each run, Pallas kernels for 10% -> 16%
where the time goes in v2:
time: 261 us; the launch traced here: 259 us
  waiting for transfers between devices  96.8 us (37%)
  Pallas kernels  55.9 us (21%)
  starting transfers between devices  49.7 us (19%)
  other arithmetic  19.9 us (8%)
  local copies, waits for them, and re-layouts  19.5 us (7%)
  between operations  15 us (6%)
  matrix products  2.64 us (1%)
    all_to_all x2, waiting for transfers between devices, to_all(): lax.all_to_all(jnp.broadcast_to(value[None], (4,) + value.shape), axis, 0...  50.2 us
    pallas_call x1, Pallas kernels, attend(): pl.pallas_call(attend_kernel, grid=(GROUP,), in_specs=[pl.BlockSpec((SEQ,...  14.6 us
    ppermute x8, starting transfers between devices, along_z(): lax.ppermute(value, ('zh', 'zl'), [(i, (i + shift) % 8) for i in range(8)])  14.4 us
    all_to_all x1, waiting for transfers between devices, shards(): rows = lax.all_to_all(rows, 'zl', 0, 0, tiled=True).reshape(SEQ, 3 * HD)  13.7 us
    pallas_call x2, Pallas kernels, back(): pl.pallas_call(kernel, in_specs=[smem(), whole((4, PAIR, 2 * HD))] + [any...  13.3 us
    ppermute x8, waiting for transfers between devices, along_z(): lax.ppermute(value, ('zh', 'zl'), [(i, (i + shift) % 8) for i in range(8)])  11.5 us
    all_to_all x1, starting transfers between devices, shards(): pieces = lax.all_to_all(pieces, DP + ('zl',), 0, 0, tiled=True)  9.88 us
    all_to_all x1, waiting for transfers between devices, shards(): lax.all_to_all(grads.reshape(4, PAIR, 2 * HD), 'zl', 0, 0, tiled=True)  9.64 us
  transfers between devices with their start and end apart: 21, of which 9 were waited for; matrix products, arithmetic and copies ran while one was open for 12% of the time, Pallas kernels for 16%

profile of v2, /device:TPU:1, one launch (start us, length us, event | category | flops | bytes accessed | tf_op | source)
XLA Modules:
  0.0 259.4 jit_solution(17105168452120972788)
XLA Ops:
  7.2 0.9 constant_dynamic-slice_fusion.2
  8.1 0.8 constant_dynamic-slice_fusion
  8.9 6.5 %collective-permute-start.1 = (bf16[384,256]{1,0:T(8,128)(2,1)S(1)}, bf16[384,256]{1,0:T(8,128)(2,1)S(1)}, u32[]{:S(2)}, u32[]{:S(2)}) collective-permute-start(bf16[384,256]{1,0:T(8,128)(2,1)S(1)} %maximum_maximum_fusion), channel_id=1, source_target_pairs={{0,14},{2,0},{4,2},{6,4},{8,6},{10,8},{12,10},{14,12},{1,15},{3,1}... | collective-permute-start | bytes 589832 | tf_op jit(solution)/shard_map/ppermute | solution.py:465
  15.6 3.6 %collective-permute-start.2 = (bf16[192,256]{1,0:T(8,128)(2,1)S(1)}, bf16[192,256]{1,0:T(8,128)(2,1)S(1)}, u32[]{:S(2)}, u32[]{:S(2)}) collective-permute-start(bf16[192,256]{1,0:T(8,128)(2,1)S(1)} %pad_maximum_fusion.4), channel_id=1, source_target_pairs={{0,12},{2,14},{4,0},{6,2},{8,4},{10,6},{12,8},{14,10},{1,13},{3,15... | collective-permute-start | bytes 294920 | tf_op jit(solution)/shard_map/ppermute | solution.py:465
  19.2 4.7 %collective-permute-done.3 = bf16[192,256]{1,0:T(8,128)(2,1)S(1)} collective-permute-done((bf16[192,256]{1,0:T(8,128)(2,1)S(1)}, bf16[192,256]{1,0:T(8,128)(2,1)S(1)}, u32[]{:S(2)}, u32[]{:S(2)}) %collective-permute-start.3) | collective-permute-done | bytes 98336 | tf_op jit(solution)/shard_map/ppermute | solution.py:465
  24.0 0.8 slice.61
  24.8 3.2 %collective-permute-start = (bf16[128,8192]{1,0:T(8,128)(2,1)}, bf16[128,8192]{1,0:T(8,128)(2,1)}, u32[]{:S(2)}, u32[]{:S(2)}) collective-permute-start(bf16[128,8192]{1,0:T(8,128)(2,1)} %param.8), channel_id=1, source_target_pairs={{0,1},{1,0},{2,3},{3,2},{4,5},{5,4},{6,7},{7,6},{8,9},{9,8},{10,11... | collective-permute-start | bytes 6291464 | tf_op jit(solution)/shard_map/ppermute | solution.py:505
  29.2 1.2 fusion.5
  30.4 1.0 collective-permute-start.5
  31.4 1.2 collective-permute-start.7
  32.7 0.9 broadcast_in_dim.8
  33.6 4.2 %all-to-all-start = ((bf16[4,128,768]{2,1,0:T(8,128)(2,1)}), bf16[4,128,768]{2,1,0:T(8,128)(2,1)S(1)}, u32[]{:S(2)}, u32[]{:S(2)}) async-start(bf16[4,128,768]{2,1,0:T(8,128)(2,1)} %broadcast_in_dim.8), calls=%async_computation | async-start | bytes 1572864 | tf_op jit(solution)/shard_map/all_to_all | solution.py:469
  37.8 3.0 %fusion.6 = (f32[1024,64]{1,0:T(8,128)}, f32[1024,64]{1,0:T(8,128)}, f32[1024,64]{1,0:T(8,128)}) fusion(f32[64]{0:T(128)S(1)} %negate_power_fusion), kind=kLoop, calls=%fused_computation.12 | loop fusion | flops 131072 | bytes 786688 | tf_op jit(solution)/shard_map/sin | solution.py:37
  40.8 14.8 %all-to-all-done = bf16[4,128,768]{2,1,0:T(8,128)(2,1)S(1)} async-done(((bf16[4,128,768]{2,1,0:T(8,128)(2,1)}), bf16[4,128,768]{2,1,0:T(8,128)(2,1)S(1)}, u32[]{:S(2)}, u32[]{:S(2)}) %all-to-all-start) | async-done | bytes 786464 | tf_op jit(solution)/shard_map/all_to_all | solution.py:469
  55.6 2.0 broadcast_in_dim.10
  57.6 4.0 %all-to-all-start.1 = ((bf16[4,512,768]{2,1,0:T(8,128)(2,1)}), bf16[4,512,768]{2,1,0:T(8,128)(2,1)S(1)}, u32[]{:S(2)}, u32[]{:S(2)}) async-start(bf16[4,512,768]{2,1,0:T(8,128)(2,1)} %broadcast_in_dim.10), calls=%async_computation.1 | async-start | bytes 6291456 | tf_op jit(solution)/shard_map/all_to_all | solution.py:469
  61.5 1.9 fusion.9
  63.5 1.1 slice.63
  64.6 0.7 pad_add_fusion.place
  65.3 2.0 slice.64
  67.3 1.9 collective-permute-start.8
  69.2 0.7 slice_bitcast_fusion
  69.9 0.7 slice_bitcast_fusion.2
  70.6 6.7 %collective-permute-done.6.two_a = bf16[1056,256]{1,0:T(8,128)(2,1)S(1)} collective-permute-done((bf16[1056,256]{1,0:T(8,128)(2,1)S(1)}, bf16[1056,256]{1,0:T(8,128)(2,1)S(1)}, u32[]{:S(2)}, u32[]{:S(2)}) %collective-permute-start.6) | collective-permute-done | bytes 540704 | tf_op jit(solution)/shard_map/ppermute | solution.py:465
  77.4 0.7 pad_maximum_fusion.5.ups
  78.2 4.6 %maximum_select_fusion.pair.hid = bf16[256,8192]{1,0:T(8,128)(2,1)S(1)} fusion(bf16[128,8192]{1,0:T(8,128)(2,1)} %collective-permute-done, bf16[128,8192]{1,0:T(8,128)(2,1)} %param.8, pred[]{:T(512)S(6)} %eq.3), kind=kLoop, calls=%fused_computation.3 | loop fusion | flops 18874368 | bytes 8388609 | tf_op jit(solution)/shard_map/jit(_where)/select_n | solution.py:506
  82.8 2.1 copy-done
  84.8 1.3 convolution_convert_fusion
  86.2 0.7 copy.16.down
  86.9 35.4 %all-to-all-done.1 = bf16[4,512,768]{2,1,0:T(8,128)(2,1)S(1)} async-done(((bf16[4,512,768]{2,1,0:T(8,128)(2,1)}), bf16[4,512,768]{2,1,0:T(8,128)(2,1)S(1)}, u32[]{:S(2)}, u32[]{:S(2)}) %all-to-all-start.1) | async-done | bytes 3145760 | tf_op jit(solution)/shard_map/all_to_all | solution.py:469
  122.3 0.7 broadcast_in_dim.11
  123.0 3.6 %all-to-all-start.3 = ((bf16[4,256,32]{1,2,0:T(8,128)(2,1)}), bf16[4,256,32]{1,2,0:T(8,128)(2,1)S(1)}, u32[]{:S(2)}, u32[]{:S(2)}) async-start(bf16[4,256,32]{1,2,0:T(8,128)(2,1)} %broadcast_in_dim.11), calls=%async_computation.3 | async-start | bytes 131072 | tf_op jit(solution)/shard_map/all_to_all | solution.py:510
  126.7 6.8 %project_line.1.so_far = f32[256,1024]{1,0:T(8,128)} custom-call(bf16[256,8192]{1,0:T(8,128)(2,1)} %copy-done, bf16[8192,128]{1,0:T(8,128)(2,1)} %own_key.7, bf16[8192,128]{1,0:T(8,128)(2,1)} %own_val.7, bf16[2048,768]{1,0:T(8,128)(2,1)} %bitcast.26, bf16[2080,256]{1,0:T(8,128)(2,1)} %collective-permute-done.5.one, bf16[1056,256]{1,0:T(8,128)(2,1)} %copy-done.6, ...), custom_call_target="tpu_custom_call" | custom-call | flops 2147483648 | bytes 11534336 | tf_op jit(solution)/shard_map/project_line/pallas_call | solution.py:140
  133.6 7.6 %project.1 = bf16[4,256,384]{2,1,0:T(8,128)(2,1)} custom-call(s32[2]{0:T(128)} %pad_add_fusion.place, bf16[256,8192]{1,0:T(8,128)(2,1)} %copy-done, bf16[8192,128]{1,0:T(8,128)(2,1)} %own_key.7, bf16[8192,128]{1,0:T(8,128)(2,1)} %own_val.7, bf16[4096,768]{1,0:T(8,128)(2,1)} %all-gather.3.cloned.1.call-done.far, f32[256,1024]{1,0:T(8,128)} %project_line.1.so_far, ...), custom_call_target="tpu_custom_call" | custom-call | flops 2147483648 | bytes 14680064 | tf_op jit(solution)/shard_map/project/pallas_call | solution.py:181
  141.2 4.7 %all-to-all-start.2 = ((bf16[4,256,384]{2,1,0:T(8,128)(2,1)}), bf16[4,256,384]{2,1,0:T(8,128)(2,1)}, u32[]{:S(2)}, u32[]{:S(2)}) async-start(bf16[4,256,384]{2,1,0:T(8,128)(2,1)} %project.1), calls=%async_computation.2 | async-start | bytes 1572864 | tf_op jit(solution)/shard_map/all_to_all | solution.py:521
  145.9 2.6 pad_maximum_fusion.1
  148.4 1.3 fusion.3
  149.7 0.5 fusion.12
  150.3 0.8 copy.17
  151.1 13.7 %all-to-all-done.2 = bf16[4,256,384]{2,1,0:T(8,128)(2,1)} async-done(((bf16[4,256,384]{2,1,0:T(8,128)(2,1)}), bf16[4,256,384]{2,1,0:T(8,128)(2,1)}, u32[]{:S(2)}, u32[]{:S(2)}) %all-to-all-start.2) | async-done | bytes 786464 | tf_op jit(solution)/shard_map/all_to_all | solution.py:521
  164.8 14.6 %attend.1 = (bf16[1024,256]{1,0:T(8,128)(2,1)}, f32[32,128]{1,0:T(8,128)}, f32[8,128]{1,0:T(8,128)}) custom-call(bf16[1024,512]{1,0:T(8,128)(2,1)} %query.1, bf16[1024,512]{1,0:T(8,128)(2,1)} %grad.1, bf16[1024,384]{1,0:T(8,128)(2,1)} %bitcast.9.rows, f32[1,128]{1,0:T(1,128)} %get-tuple-element.19.col_scale, bf16[1024,32]{1,0:T(8,128)(2,1)} %bitcast.31, ...), custom_call_target="tpu_custom_call" | custom-call | flops 5368709120 | bytes 6291456 | tf_op jit(solution)/shard_map/attend/pallas_call | solution.py:255
  179.5 0.7 broadcast_divide_fusion
  180.2 0.7 pad_maximum_fusion.6
  180.9 3.5 %all-to-all-start.4 = ((bf16[4,256,256]{2,1,0:T(8,128)(2,1)}), bf16[4,256,256]{2,1,0:T(8,128)(2,1)S(1)}, u32[]{:S(2)}, u32[]{:S(2)}) async-start(bf16[4,256,256]{2,1,0:T(8,128)(2,1)} %bitcast.30), calls=%async_computation.4 | async-start | bytes 1048576 | tf_op jit(solution)/shard_map/all_to_all | solution.py:523
  184.4 3.1 %collective-permute-done.12 = f32[40,128]{1,0:T(8,128)S(1)} collective-permute-done((f32[40,128]{1,0:T(8,128)S(1)}, f32[40,128]{1,0:T(8,128)S(1)}, u32[]{:S(2)}, u32[]{:S(2)}) %collective-permute-start.12) | collective-permute-done | bytes 20512 | tf_op jit(solution)/shard_map/ppermute | solution.py:525
  187.5 0.7 fusion.11
  188.2 0.6 pad.9
  188.8 9.6 %all-to-all-done.4.grads = bf16[4,256,256]{2,1,0:T(8,128)(2,1)S(1)} async-done(((bf16[4,256,256]{2,1,0:T(8,128)(2,1)}), bf16[4,256,256]{2,1,0:T(8,128)(2,1)S(1)}, u32[]{:S(2)}, u32[]{:S(2)}) %all-to-all-start.4) | async-done | bytes 524320 | tf_op jit(solution)/shard_map/all_to_all | solution.py:523
  198.5 0.8 copy-done.3
  199.3 1.9 rank_part.1
  201.2 1.5 collective-permute-start.9
  202.7 1.2 collective-permute-done.9
  203.9 1.5 add_convert_fusion.rank
  205.4 4.6 %down_part.1._ = bf16[1024,128]{1,0:T(8,128)(2,1)} custom-call(s32[2]{0:T(128)} %pad_add_fusion.place, bf16[256,32]{1,0:T(8,128)(2,1)} %add_convert_fusion.rank, bf16[256,8192]{1,0:T(8,128)(2,1)} %copy-done), custom_call_target="tpu_custom_call" | custom-call | flops 134217728 | bytes 5242880 | tf_op jit(solution)/shard_map/down_part/pallas_call | solution.py:392
  210.0 6.7 %back_line.1 = (bf16[128,4096]{1,0:T(8,128)(2,1)}, bf16[128,4096]{1,0:T(8,128)(2,1)}) custom-call(s32[2]{0:T(128)} %pad_add_fusion.place, bf16[4,256,256]{2,1,0:T(8,128)(2,1)} %copy-done.3, bf16[8192,128]{1,0:T(8,128)(2,1)} %own_key.7, bf16[8192,128]{1,0:T(8,128)(2,1)} %own_val.7, bf16[2048,768]{1,0:T(8,128)(2,1)} %bitcast.27, ...), custom_call_target="tpu_custom_call" | custom-call | flops 1048576 | bytes 1048576 | tf_op jit(solution)/shard_map/back_line/pallas_call | solution.py:355
  217.2 6.6 %back_near.1 = (bf16[128,4096]{1,0:T(8,128)(2,1)}, bf16[128,4096]{1,0:T(8,128)(2,1)}) custom-call(s32[2]{0:T(128)} %pad_add_fusion.place, bf16[4,256,256]{2,1,0:T(8,128)(2,1)} %copy-done.3, bf16[8192,128]{1,0:T(8,128)(2,1)} %own_key.7, bf16[8192,128]{1,0:T(8,128)(2,1)} %own_val.7, bf16[4096,768]{1,0:T(8,128)(2,1)} %all-gather.3.cloned.1.call-done.far, ...), custom_call_target="tpu_custom_call" | custom-call | flops 1048576 | bytes 1048576 | tf_op jit(solution)/shard_map/back_near/pallas_call | solution.py:355
  224.0 9.9 %all-to-all-start.5 = ((bf16[128,8,128]{2,1,0:T(8,128)(2,1)}), bf16[128,8,128]{2,1,0:T(8,128)(2,1)S(1)}, u32[]{:S(2)}, u32[]{:S(2)}) async-start(bf16[128,8,128]{2,1,0:T(8,128)(2,1)} %bitcast.13), calls=%async_computation.5 | async-start | bytes 524288 | tf_op jit(solution)/shard_map/all_to_all | solution.py:537
  234.0 1.0 copy-done.10
  235.3 5.2 %join.1._ = bf16[128,8192]{1,0:T(8,128)(2,1)} custom-call(s32[2]{0:T(128)} %pad_add_fusion.place, bf16[256,32]{1,0:T(8,128)(2,1)} %add_convert_fusion.rank, bf16[128,4096]{1,0:T(8,128)(2,1)} %get-tuple-element.12.mine_a, bf16[128,4096]{1,0:T(8,128)(2,1)} %copy-done.11, bf16[128,4096]{1,0:T(8,128)(2,1)} %get-tuple-element.14.mine_b, ...), custom_call_target="tpu_custom_call" | custom-call | flops 1048576 | bytes 1048576 | tf_op jit(solution)/shard_map/join/pallas_call | solution.py:451
  240.6 7.4 %all-to-all-done.5 = bf16[128,8,128]{2,1,0:T(8,128)(2,1)S(1)} async-done(((bf16[128,8,128]{2,1,0:T(8,128)(2,1)}), bf16[128,8,128]{2,1,0:T(8,128)(2,1)S(1)}, u32[]{:S(2)}, u32[]{:S(2)}) %all-to-all-start.5) | async-done | bytes 262176 | tf_op jit(solution)/shard_map/all_to_all | solution.py:537
  248.0 0.7 copy-done.9
  248.7 1.8 finish.1
  250.4 1.0 slice_reduce_fusion
  251.5 0.6 slice.69
  (59 shorter events, 2.7 us)
Async XLA Ops:
  7.2 126.4 %all-gather.3.cloned.1.call-start = ((), (), s32[]{:S(2)}) async-start(), calls=%async_computation.6 | async-start | bytes 6684672 | tf_op jit(solution)/shard_map/all_gather | solution.py:487
  8.9 15.0 %collective-permute-start.1 = (bf16[384,256]{1,0:T(8,128)(2,1)S(1)}, bf16[384,256]{1,0:T(8,128)(2,1)S(1)}, u32[]{:S(2)}, u32[]{:S(2)}) collective-permute-start(bf16[384,256]{1,0:T(8,128)(2,1)S(1)} %maximum_maximum_fusion), channel_id=1, source_target_pairs={{0,14},{2,0},{4,2},{6,4},{8,6},{10,8},{12,10},{14,12},{1,15},{3,1}... | collective-permute-start | bytes 589832 | tf_op jit(solution)/shard_map/ppermute | solution.py:465
  15.4 8.5 %collective-permute-start.4 = (bf16[384,256]{1,0:T(8,128)(2,1)S(1)}, bf16[384,256]{1,0:T(8,128)(2,1)S(1)}, u32[]{:S(2)}, u32[]{:S(2)}) collective-permute-start(bf16[384,256]{1,0:T(8,128)(2,1)S(1)} %maximum_maximum_fusion), channel_id=1, source_target_pairs={{0,2},{2,4},{4,6},{6,8},{8,10},{10,12},{12,14},{14,0},{1,3},{3,5},... | collective-permute-start | bytes 589832 | tf_op jit(solution)/shard_map/ppermute | solution.py:465
  15.4 8.5 %collective-permute-start.3 = (bf16[192,256]{1,0:T(8,128)(2,1)S(1)}, bf16[192,256]{1,0:T(8,128)(2,1)S(1)}, u32[]{:S(2)}, u32[]{:S(2)}) collective-permute-start(bf16[192,256]{1,0:T(8,128)(2,1)S(1)} %slice.60), channel_id=1, source_target_pairs={{0,4},{2,6},{4,8},{6,10},{8,12},{10,14},{12,0},{14,2},{1,5},{3,7},... | collective-permute-start | bytes 294920 | tf_op jit(solution)/shard_map/ppermute | solution.py:465
  15.5 13.7 %slice-start = ((bf16[8192,128]{1,0:T(8,128)(2,1)}), bf16[2048,128]{1,0:T(8,128)(2,1)S(1)}, s32[]{:S(2)}) async-start(bf16[8192,128]{1,0:T(8,128)(2,1)} %own_key.7), calls=%async_computation.8 | async-start | bytes 1048576 | tf_op jit(solution)/shard_map/slice | solution.py:490
  15.5 13.7 %slice-start.1 = ((bf16[8192,128]{1,0:T(8,128)(2,1)}), bf16[2048,128]{1,0:T(8,128)(2,1)S(1)}, s32[]{:S(2)}) async-start(bf16[8192,128]{1,0:T(8,128)(2,1)} %own_val.7), calls=%async_computation.9 | async-start | bytes 1048576 | tf_op jit(solution)/shard_map/slice | solution.py:490
  15.6 13.7 %copy-start.12 = (bf16[32,128]{1,0:T(8,128)(2,1)S(1)}, bf16[32,128]{1,0:T(8,128)(2,1)}, u32[]{:S(2)}) copy-start(bf16[32,128]{1,0:T(8,128)(2,1)} %param.12) | copy-start | bytes 24580
  15.6 8.3 %collective-permute-start.2 = (bf16[192,256]{1,0:T(8,128)(2,1)S(1)}, bf16[192,256]{1,0:T(8,128)(2,1)S(1)}, u32[]{:S(2)}, u32[]{:S(2)}) collective-permute-start(bf16[192,256]{1,0:T(8,128)(2,1)S(1)} %pad_maximum_fusion.4), channel_id=1, source_target_pairs={{0,12},{2,14},{4,0},{6,2},{8,4},{10,6},{12,8},{14,10},{1,13},{3,15... | collective-permute-start | bytes 294920 | tf_op jit(solution)/shard_map/ppermute | solution.py:465
  24.8 53.4 %collective-permute-start = (bf16[128,8192]{1,0:T(8,128)(2,1)}, bf16[128,8192]{1,0:T(8,128)(2,1)}, u32[]{:S(2)}, u32[]{:S(2)}) collective-permute-start(bf16[128,8192]{1,0:T(8,128)(2,1)} %param.8), channel_id=1, source_target_pairs={{0,1},{1,0},{2,3},{3,2},{4,5},{5,4},{6,7},{7,6},{8,9},{9,8},{10,11... | collective-permute-start | bytes 6291464 | tf_op jit(solution)/shard_map/ppermute | solution.py:505
  30.4 33.1 %collective-permute-start.5 = (bf16[2080,256]{1,0:T(8,128)(2,1)}, bf16[2080,256]{1,0:T(8,128)(2,1)}, u32[]{:S(2)}, u32[]{:S(2)}) collective-permute-start(bf16[2080,256]{1,0:T(8,128)(2,1)} %fusion.5), channel_id=1, source_target_pairs={{0,14},{2,0},{4,2},{6,4},{8,6},{10,8},{12,10},{14,12},{1,15},{3,1}... | collective-permute-start | bytes 3194888 | tf_op jit(solution)/shard_map/ppermute | solution.py:465
  31.4 33.9 %collective-permute-start.7 = (bf16[2080,256]{1,0:T(8,128)(2,1)}, bf16[2080,256]{1,0:T(8,128)(2,1)}, u32[]{:S(2)}, u32[]{:S(2)}) collective-permute-start(bf16[2080,256]{1,0:T(8,128)(2,1)} %fusion.5), channel_id=1, source_target_pairs={{0,2},{2,4},{4,6},{6,8},{8,10},{10,12},{12,14},{14,0},{1,3},{3,5},... | collective-permute-start | bytes 3194888 | tf_op jit(solution)/shard_map/ppermute | solution.py:465
  33.6 22.0 %all-to-all-start = ((bf16[4,128,768]{2,1,0:T(8,128)(2,1)}), bf16[4,128,768]{2,1,0:T(8,128)(2,1)S(1)}, u32[]{:S(2)}, u32[]{:S(2)}) async-start(bf16[4,128,768]{2,1,0:T(8,128)(2,1)} %broadcast_in_dim.8), calls=%async_computation | async-start | bytes 1572864 | tf_op jit(solution)/shard_map/all_to_all | solution.py:469
  57.6 64.8 %all-to-all-start.1 = ((bf16[4,512,768]{2,1,0:T(8,128)(2,1)}), bf16[4,512,768]{2,1,0:T(8,128)(2,1)S(1)}, u32[]{:S(2)}, u32[]{:S(2)}) async-start(bf16[4,512,768]{2,1,0:T(8,128)(2,1)} %broadcast_in_dim.10), calls=%async_computation.1 | async-start | bytes 6291456 | tf_op jit(solution)/shard_map/all_to_all | solution.py:469
  64.6 12.8 %collective-permute-start.6 = (bf16[1056,256]{1,0:T(8,128)(2,1)S(1)}, bf16[1056,256]{1,0:T(8,128)(2,1)S(1)}, u32[]{:S(2)}, u32[]{:S(2)}) collective-permute-start(bf16[1056,256]{1,0:T(8,128)(2,1)S(1)} %slice.63), channel_id=1, source_target_pairs={{0,14},{2,0},{4,2},{6,4},{8,6},{10,8},{12,10},{14,12},{1,15},{3,1}... | collective-permute-start | bytes 1622024 | tf_op jit(solution)/shard_map/ppermute | solution.py:465
  67.3 59.4 %collective-permute-start.8 = (bf16[1024,256]{1,0:T(8,128)(2,1)}, bf16[1024,256]{1,0:T(8,128)(2,1)}, u32[]{:S(2)}, u32[]{:S(2)}) collective-permute-start(bf16[1024,256]{1,0:T(8,128)(2,1)} %slice.64), channel_id=1, source_target_pairs={{0,2},{2,4},{4,6},{6,8},{8,10},{10,12},{12,14},{14,0},{1,3},{3,5},... | collective-permute-start | bytes 1572872 | tf_op jit(solution)/shard_map/ppermute | solution.py:465
  77.3 0.8 copy-start.6
  78.2 6.7 %copy-start.7 = (bf16[32,8192]{1,0:T(8,128)(2,1)S(1)}, bf16[32,8192]{1,0:T(8,128)(2,1)}, u32[]{:S(2)}) copy-start(bf16[32,8192]{1,0:T(8,128)(2,1)} %factor.1) | copy-start | bytes 1572868
  82.8 2.1 copy-start
  122.3 4.3 %copy-start.2 = (bf16[4,512,768]{2,1,0:T(8,128)(2,1)}, bf16[4,512,768]{2,1,0:T(8,128)(2,1)S(1)}, u32[]{:S(2)}) copy-start(bf16[4,512,768]{2,1,0:T(8,128)(2,1)S(1)} %all-to-all-done.1) | copy-start | bytes 9437188
  123.0 18.1 %all-to-all-start.3 = ((bf16[4,256,32]{1,2,0:T(8,128)(2,1)}), bf16[4,256,32]{1,2,0:T(8,128)(2,1)S(1)}, u32[]{:S(2)}, u32[]{:S(2)}) async-start(bf16[4,256,32]{1,2,0:T(8,128)(2,1)} %broadcast_in_dim.11), calls=%async_computation.3 | async-start | bytes 131072 | tf_op jit(solution)/shard_map/all_to_all | solution.py:510
  133.6 12.3 %copy-start.4 = (f32[1024,64]{1,0:T(8,128)S(1)}, f32[1024,64]{1,0:T(8,128)}, u32[]{:S(2)}) copy-start(f32[1024,64]{1,0:T(8,128)} %get-tuple-element.20) | copy-start | bytes 786436
  133.6 12.3 %copy-start.5 = (f32[1024,64]{1,0:T(8,128)S(1)}, f32[1024,64]{1,0:T(8,128)}, u32[]{:S(2)}) copy-start(f32[1024,64]{1,0:T(8,128)} %get-tuple-element.21) | copy-start | bytes 786436
  141.2 7.3 %copy-start.1 = (bf16[8192,128]{1,0:T(8,128)(2,1)S(1)}, bf16[8192,128]{1,0:T(8,128)(2,1)}, u32[]{:S(2)}) copy-start(bf16[8192,128]{1,0:T(8,128)(2,1)} %own_val.7) | copy-start | bytes 6291460
  141.2 23.6 %all-to-all-start.2 = ((bf16[4,256,384]{2,1,0:T(8,128)(2,1)}), bf16[4,256,384]{2,1,0:T(8,128)(2,1)}, u32[]{:S(2)}, u32[]{:S(2)}) async-start(bf16[4,256,384]{2,1,0:T(8,128)(2,1)} %project.1), calls=%async_computation.2 | async-start | bytes 1572864 | tf_op jit(solution)/shard_map/all_to_all | solution.py:521
  145.9 2.6 copy-start.8
  148.4 1.3 copy-start.13
  180.9 6.6 %collective-permute-start.12 = (f32[40,128]{1,0:T(8,128)S(1)}, f32[40,128]{1,0:T(8,128)S(1)}, u32[]{:S(2)}, u32[]{:S(2)}) collective-permute-start(f32[40,128]{1,0:T(8,128)S(1)} %pad_maximum_fusion.6), channel_id=1, source_target_pairs={{0,8},{8,0},{1,9},{9,1},{2,10},{10,2},{3,11},{11,3},{4,12},{12,4},... | collective-permute-start | bytes 61448 | tf_op jit(solution)/shard_map/ppermute | solution.py:525
  180.9 17.6 %all-to-all-start.4 = ((bf16[4,256,256]{2,1,0:T(8,128)(2,1)}), bf16[4,256,256]{2,1,0:T(8,128)(2,1)S(1)}, u32[]{:S(2)}, u32[]{:S(2)}) async-start(bf16[4,256,256]{2,1,0:T(8,128)(2,1)} %bitcast.30), calls=%async_computation.4 | async-start | bytes 1048576 | tf_op jit(solution)/shard_map/all_to_all | solution.py:523
  184.4 66.1 %all-gather.5.cloned.1.call-start = ((), (), s32[]{:S(2)}) async-start(), calls=%async_computation.7 | async-start | bytes 1114112 | tf_op jit(solution)/shard_map/all_gather | solution.py:526
  198.5 0.8 copy-start.3
  201.2 2.7 %collective-permute-start.9 = (f32[256,32]{1,0:T(8,128)}, f32[256,32]{1,0:T(8,128)S(1)}, u32[]{:S(2)}, u32[]{:S(2)}) collective-permute-start(f32[256,32]{1,0:T(8,128)} %rank_part.1), channel_id=1, source_target_pairs={{0,1},{1,0},{2,3},{3,2},{4,5},{5,4},{6,7},{7,6},{8,9},{9,8},{10,11... | collective-permute-start | bytes 98312 | tf_op jit(solution)/shard_map/ppermute | solution.py:529
  216.8 17.2 %collective-permute-start.11 = (bf16[128,4096]{1,0:T(8,128)(2,1)}, bf16[128,4096]{1,0:T(8,128)(2,1)S(1)}, u32[]{:S(2)}, u32[]{:S(2)}) collective-permute-start(bf16[128,4096]{1,0:T(8,128)(2,1)} %get-tuple-element.15), channel_id=1, source_target_pairs={{0,1},{1,0},{2,3},{3,2},{4,5},{5,4},{6,7},{7,6},{8,9},{9,8},{10,11... | collective-permute-start | bytes 3145736 | tf_op jit(solution)/shard_map/ppermute | solution.py:536
  223.8 10.2 %collective-permute-start.10 = (bf16[128,4096]{1,0:T(8,128)(2,1)}, bf16[128,4096]{1,0:T(8,128)(2,1)S(1)}, u32[]{:S(2)}, u32[]{:S(2)}) collective-permute-start(bf16[128,4096]{1,0:T(8,128)(2,1)} %get-tuple-element.13), channel_id=1, source_target_pairs={{0,1},{1,0},{2,3},{3,2},{4,5},{5,4},{6,7},{7,6},{8,9},{9,8},{10,11... | collective-permute-start | bytes 3145736 | tf_op jit(solution)/shard_map/ppermute | solution.py:532
  224.0 23.9 %all-to-all-start.5 = ((bf16[128,8,128]{2,1,0:T(8,128)(2,1)}), bf16[128,8,128]{2,1,0:T(8,128)(2,1)S(1)}, u32[]{:S(2)}, u32[]{:S(2)}) async-start(bf16[128,8,128]{2,1,0:T(8,128)(2,1)} %bitcast.13), calls=%async_computation.5 | async-start | bytes 524288 | tf_op jit(solution)/shard_map/all_to_all | solution.py:537
  233.9 1.0 copy-start.10
  234.0 1.4 copy-start.11
  248.0 0.7 copy-start.9
Sparse Core Ops, SparseCore 0:
  24.9 94.4 all-gather.2
  189.0 44.8 all-gather.4
